TPU v7x, 256 devices: a whole 4x4x8 slice. The times are simulated.
256 devices in a mesh: seq: 32 (over z, x_hi, core), head: 8 (over x_lo, y).
Axes of the slice: x: 4 (x_hi: 2, x_lo: 2; x = x_hi * 2 + x_lo), y: 4, z: 8, core: 2. Of those that a mesh axis runs over, the one named last changes fastest.
Arguments:
- queries: bfloat16 [128, 2, 8192], P('seq', None, 'head'), may hold values from -7 to 7
- prefix_keys: bfloat16 [131072, 8, 128], P('seq', 'head'), may hold values from -15 to 15
- prefix_values: bfloat16 [131072, 8, 128], P('seq', 'head'), may hold values from -12 to 12
- suffix_keys: bfloat16 [128, 4096, 8, 128], P('seq', None, 'head'), may hold values from -19 to 19
- suffix_values: bfloat16 [128, 4096, 8, 128], P('seq', None, 'head'), may hold values from -12 to 12
- new_keys: bfloat16 [128, 2, 8, 128], P('seq', None, 'head'), may hold values from -8 to 8
- new_values: bfloat16 [128, 2, 8, 128], P('seq', None, 'head'), may hold values from -12 to 12
- suffix_lengths: int32 [128], P('seq'), may hold values from 1 to 4096, 262144 in all
- out_weight: bfloat16 [8192, 8192], P('head', 'seq'), may hold values from -0.0625 to 0.0625
Outputs:
- layer_output: bfloat16 [128, 2, 8192], P('head', None, 'seq')
Inputs may be any that keep to these rules, and one draw needn't show every extreme that they name: `suffix_lengths`: the longest suffix holds exactly 4096 tokens.
All inputs are finite; a program needn't handle non-finite values. No bound on the sum of `suffix_lengths` on one device may be relied on, other than what follows from the above.
Results may differ from a plain program's by a relative error of at most 0.015.
Values may be sent and summed in bfloat16 or wider, within the bound.
No kernel may reach another device: no remote copies, remote signals or barrier semaphores. Data moves between devices by JAX's collectives and lax.ppermute only.
A program may use at most 192 MiB of HBM per device.

v0:
```python
import functools

import jax
import jax.numpy as jnp
from jax import lax
from jax.experimental import pallas as pl
from jax.experimental.pallas import tpu as pltpu
from jax.sharding import PartitionSpec as P

LOW = -1.0e30
LOG2E = 1.4426950408889634
STAT_ROWS = 16
TOTAL_MAX = 2.0**100


def dot_rows(left, right):
    return lax.dot_general(
        left, right, (((1,), (1,)), ((), ())), preferred_element_type=jnp.float32
    )


def split_bf16(value):
    high = value.astype(jnp.bfloat16)
    rest = value - high.astype(jnp.float32)
    middle = rest.astype(jnp.bfloat16)
    low = (rest - middle.astype(jnp.float32)).astype(jnp.bfloat16)
    return high, middle, low


def running_softmax(query_rows, key_refs, value_refs, key_block, scale):
    count, head_dim = query_rows.shape

    def advance(key_ref, value_ref):
        def step(index, state):
            top, total, acc = state
            rows = pl.ds(pl.multiple_of(index * key_block, key_block), key_block)
            scores = dot_rows(query_rows, key_ref[rows, :]) * scale
            new_top = jnp.maximum(top, jnp.max(scores, axis=1, keepdims=True))
            weights = jnp.exp2(scores - new_top)
            rescale = jnp.exp2(top - new_top)
            total = total * rescale + jnp.sum(weights, axis=1, keepdims=True)
            acc = acc * rescale + jnp.dot(
                weights.astype(jnp.bfloat16), value_ref[rows, :], preferred_element_type=jnp.float32
            )
            return new_top, total, acc

        return step

    state = (
        jnp.full((count, 1), LOW, jnp.float32),
        jnp.zeros((count, 1), jnp.float32),
        jnp.zeros((count, head_dim), jnp.float32),
    )
    for key_ref, value_ref in zip(key_refs, value_refs):
        state = lax.fori_loop(
            0, key_ref.shape[0] // key_block, advance(key_ref, value_ref), state
        )
    return state


def shifted_softmax(query_rows, key_ref, value_ref, key_block, scale, top, acc):
    ones = jnp.ones((key_block, query_rows.shape[1]), jnp.bfloat16)
    spans = [slice(start, start + key_block) for start in range(0, key_ref.shape[0], key_block)]

    def score(span):
        return dot_rows(query_rows, key_ref[span, :]) * scale

    scores = score(spans[0])
    for index, span in enumerate(spans):
        later = score(spans[index + 1]) if index + 1 < len(spans) else None
        if top is None:
            top = jnp.max(scores, axis=1, keepdims=True)
        weights = jnp.exp2(scores - top).astype(jnp.bfloat16)
        values = jnp.concatenate([value_ref[span, :], ones], axis=1)
        part = jnp.dot(weights, values, preferred_element_type=jnp.float32)
        acc = part if acc is None else acc + part
        scores = later
    return top, acc


def first_kernel(query_ref, key_ref, value_ref, top_ref, state_ref, *, key_block, scale):
    top, acc = shifted_softmax(query_ref[...], key_ref, value_ref, key_block, scale, None, None)
    top_ref[...] = jnp.broadcast_to(top, top_ref.shape)
    state_ref[...] = acc


def second_kernel(
    query_ref, key_ref, value_ref, other_key_ref, other_value_ref, first_top_ref, state_ref, out_ref,
    top_ref, total_ref, acc_ref, *, key_block, group, scale,
):
    query_rows = query_ref[...]
    count, head_dim = query_rows.shape
    top = first_top_ref[...]
    wide = jnp.concatenate([top] * (key_block // head_dim), axis=1)
    _, acc = shifted_softmax(
        query_rows, key_ref, value_ref, key_block, scale, wide, state_ref[...]
    )
    total = acc[:, head_dim:]
    top_ref[...] = top
    total_ref[...] = total
    acc_ref[...] = acc[:, :head_dim]

    @pl.when(jnp.logical_not(jnp.max(total) < TOTAL_MAX))
    def _():
        top, total, acc = running_softmax(
            query_rows, (other_key_ref, key_ref), (other_value_ref, value_ref), key_block, scale
        )
        top_ref[...] = jnp.broadcast_to(top, (count, head_dim))
        total_ref[...] = jnp.broadcast_to(total, (count, head_dim))
        acc_ref[...] = acc

    row = lax.broadcasted_iota(jnp.int32, (group, head_dim), 0)
    lane = lax.broadcasted_iota(jnp.int32, (group, head_dim), 1)
    tile_row = lax.broadcasted_iota(jnp.int32, (STAT_ROWS, head_dim), 0)
    for index in range(count // group):
        rows = slice(index * group, (index + 1) * group)
        total = total_ref[rows, :]
        stat = jnp.where(lane == row, top_ref[rows, :], 0.0)
        stat = jnp.where(lane == row + group, total, stat)
        high, middle, low = split_bf16(jnp.sum(stat, axis=0, keepdims=True))
        out_ref[index, :group, :] = (acc_ref[rows, :] / total).astype(jnp.bfloat16)
        tile = jnp.where(tile_row == 0, high.astype(jnp.float32), 0.0)
        tile = jnp.where(tile_row == 1, middle.astype(jnp.float32), tile)
        tile = jnp.where(tile_row == 2, low.astype(jnp.float32), tile)
        out_ref[index, group:, :] = tile.astype(jnp.bfloat16)


def prefix_parts(query_rows, keys, values, other_keys, other_values, group, scale):
    count, head_dim = query_rows.shape
    positions = keys.shape[0]
    held = pl.BlockSpec(memory_space=pltpu.VMEM)
    limit = pltpu.CompilerParams(vmem_limit_bytes=32 * 2**20)
    key_block = min(256, positions)
    cost = pl.CostEstimate(
        flops=6 * count * positions * head_dim,
        bytes_accessed=4 * positions * head_dim,
        transcendentals=count * positions,
    )
    top, state = pl.pallas_call(
        functools.partial(first_kernel, key_block=key_block, scale=scale),
        in_specs=[held] * 3,
        out_specs=[held] * 2,
        out_shape=[
            jax.ShapeDtypeStruct((count, head_dim), jnp.float32),
            jax.ShapeDtypeStruct((count, 2 * head_dim), jnp.float32),
        ],
        compiler_params=limit,
        cost_estimate=cost,
        name="prefix_first",
    )(query_rows, other_keys, other_values)
    return pl.pallas_call(
        functools.partial(second_kernel, key_block=key_block, group=group, scale=scale),
        in_specs=[held] * 7,
        out_specs=held,
        out_shape=jax.ShapeDtypeStruct(
            (count // group, group + STAT_ROWS, head_dim), jnp.bfloat16
        ),
        scratch_shapes=[pltpu.VMEM((count, head_dim), jnp.float32)] * 3,
        compiler_params=limit,
        cost_estimate=cost,
        name="prefix_second",
    )(query_rows, keys, values, other_keys, other_values, top, state)


def suffix_kernel(
    length_ref, query_ref, new_key_ref, new_value_ref, key_ref, value_ref,
    mean_ref, top_ref, total_ref, key_held, value_held, sems, *, key_block, group_size, scale,
):
    requests, rows, head_dim = query_ref.shape
    blocks = key_ref.shape[1] // key_block
    pair = 2 if requests % 2 == 0 else 1

    def copies(request, block):
        span = pl.ds(block * key_block, key_block)
        return [
            pltpu.make_async_copy(
                source.at[request, span, :], target.at[request, span, :], sems.at[kind, request, block]
            )
            for kind, (source, target) in enumerate(((key_ref, key_held), (value_ref, value_held)))
        ]

    def filled(start, block):
        longest = length_ref[start]
        for request in range(start + 1, start + pair):
            longest = jnp.maximum(longest, length_ref[request])
        return block * key_block < longest

    def absorb(request, block, top, total, acc):
        span = pl.ds(block * key_block, key_block)
        scores = dot_rows(query_ref[request], key_held[request, span, :]) * scale
        slot = block * key_block + lax.broadcasted_iota(jnp.int32, scores.shape, 1)
        scores = jnp.where(slot < length_ref[request], scores, LOW)
        new_top = jnp.maximum(top, jnp.max(scores, axis=1, keepdims=True))
        weights = jnp.exp2(scores - new_top)
        rescale = jnp.exp2(top - new_top)
        total = total * rescale + jnp.sum(weights, axis=1, keepdims=True)
        acc = acc * rescale + jnp.dot(
            weights.astype(jnp.bfloat16),
            value_held[request, span, :],
            preferred_element_type=jnp.float32,
        )
        return new_top, total, acc

    def keep(request, top, total, acc):
        mean_ref[request] = acc
        top_ref[request] = jnp.broadcast_to(top, (rows, head_dim))
        total_ref[request] = jnp.broadcast_to(total, (rows, head_dim))

    for request in range(requests):
        for copy in copies(request, 0):
            copy.start()
    for block in range(1, blocks):
        for start in range(0, requests, pair):

            @pl.when(filled(start, block))
            def _(start=start, block=block):
                for request in range(start, start + pair):
                    for copy in copies(request, block):
                        copy.start()

    for request in range(requests):
        for copy in copies(request, 0):
            copy.wait()
    states = []
    for request in range(requests):
        count = new_key_ref.shape[1]
        scores = dot_rows(query_ref[request], new_key_ref[request]) * scale
        step = lax.broadcasted_iota(jnp.int32, (rows, count), 0) // group_size
        slot = lax.broadcasted_iota(jnp.int32, (rows, count), 1)
        allowed = step >= slot
        top = jnp.max(jnp.where(allowed, scores, LOW), axis=1, keepdims=True)
        weights = jnp.where(allowed, jnp.exp2(scores - top), 0.0)
        rounded = weights.astype(jnp.bfloat16).astype(jnp.float32)
        values = new_value_ref[request].astype(jnp.float32)
        acc = rounded[:, 0:1] * values[0:1]
        for index in range(1, count):
            acc = acc + rounded[:, index : index + 1] * values[index : index + 1]
        total = jnp.sum(weights, axis=1, keepdims=True)
        states.append(absorb(request, 0, top, total, acc))
    for request in range(requests):
        keep(request, *states[request])

    for block in range(1, blocks):
        for start in range(0, requests, pair):

            @pl.when(filled(start, block))
            def _(start=start, block=block):
                members = range(start, start + pair)
                for request in members:
                    for copy in copies(request, block):
                        copy.wait()
                states = [
                    absorb(
                        request, block, top_ref[request][:, 0:1], total_ref[request][:, 0:1],
                        mean_ref[request],
                    )
                    for request in members
                ]
                for request, state in zip(members, states):
                    keep(request, *state)

    mean_ref[...] = mean_ref[...] / total_ref[...]


def suffix_part(query_rows, keys, values, new_keys, new_values, lengths, group_size, scale):
    requests, rows, head_dim = query_rows.shape
    slots = keys.shape[1]
    key_block = min(2048, slots)
    held = pl.BlockSpec(memory_space=pltpu.VMEM)
    away = pl.BlockSpec(memory_space=pltpu.HBM)
    return pl.pallas_call(
        functools.partial(suffix_kernel, key_block=key_block, group_size=group_size, scale=scale),
        in_specs=[pl.BlockSpec(memory_space=pltpu.SMEM), held, held, held, away, away],
        out_specs=[held] * 3,
        out_shape=[jax.ShapeDtypeStruct((requests, rows, head_dim), jnp.float32)] * 3,
        scratch_shapes=[pltpu.VMEM(keys.shape, keys.dtype)] * 2
        + [pltpu.SemaphoreType.DMA((2, requests, slots // key_block))],
        compiler_params=pltpu.CompilerParams(vmem_limit_bytes=52 * 2**20),
        cost_estimate=pl.CostEstimate(
            flops=4 * requests * rows * slots * head_dim,
            bytes_accessed=4 * requests * slots * head_dim,
            transcendentals=requests * rows * slots,
        ),
        name="suffix_part",
    )(lengths, query_rows, new_keys, new_values, keys, values)


def combine_kernel(part_ref, mean_ref, top_ref, total_ref, out_ref, acc_ref):
    senders, height, head_dim = part_ref.shape
    rows = height - STAT_ROWS
    lines = out_ref.shape[0]
    heads = rows // lines
    stat = jnp.sum(part_ref[:, rows : rows + STAT_ROWS, :].astype(jnp.float32), axis=1)
    stat = stat.T
    own_top = top_ref[...][:, 0:1]
    own_total = total_ref[...][:, 0:1]
    tops, totals = stat[:rows], stat[rows : 2 * rows]
    peak = jnp.maximum(jnp.max(tops, axis=1, keepdims=True), own_top)
    weights = jnp.exp2(tops - peak) * totals
    own = jnp.exp2(own_top - peak) * own_total
    total = jnp.sum(weights, axis=1, keepdims=True) + own
    acc = mean_ref[...] * own
    for sender in range(senders):
        acc = acc + part_ref[sender, :rows, :].astype(jnp.float32) * weights[:, sender : sender + 1]
    acc_ref[...] = acc / total
    for head in range(heads):
        out_ref[:, head * head_dim : (head + 1) * head_dim] = acc_ref[
            pl.ds(head, lines, stride=heads), :
        ].astype(jnp.bfloat16)


def combine(parts, mean, top, total, lines):
    rows, head_dim = mean.shape
    held = pl.BlockSpec(memory_space=pltpu.VMEM)
    return pl.pallas_call(
        combine_kernel,
        in_specs=[held] * 4,
        out_specs=held,
        out_shape=jax.ShapeDtypeStruct((lines, rows // lines * head_dim), jnp.bfloat16),
        scratch_shapes=[pltpu.VMEM((rows, head_dim), jnp.float32)],
        compiler_params=pltpu.CompilerParams(vmem_limit_bytes=16 * 2**20),
        name="combine_parts",
    )(parts, mean, top, total)


def shards(
    queries, prefix_keys, prefix_values, suffix_keys, suffix_values, new_keys, new_values,
    suffix_lengths, out_weight,
):
    owned, steps, row_width = queries.shape
    head_dim = prefix_keys.shape[2]
    group_size = row_width // head_dim
    group = owned * steps * group_size
    scale = head_dim**-0.5 * LOG2E
    everyone = owned * lax.axis_size("seq")
    devices = lax.axis_size("seq")
    sharers = devices // 2
    same_core = [list(range(core, devices, 2)) for core in range(2)]
    swap_cores = [(index, index ^ 1) for index in range(devices)]
    own_rows = lax.optimization_barrier(queries.reshape(group, head_dim))
    keys, values = prefix_keys[:, 0, :], prefix_values[:, 0, :]
    gathered = lax.all_to_all(
        jnp.tile(own_rows, (sharers, 1)), "seq", 0, 0, axis_index_groups=same_core, tiled=True
    )
    other_keys = lax.ppermute(keys, "seq", swap_cores)
    other_values = lax.ppermute(values, "seq", swap_cores)
    mean, top, total = suffix_part(
        own_rows.reshape(owned, steps * group_size, head_dim),
        suffix_keys[:, :, 0, :], suffix_values[:, :, 0, :],
        new_keys[:, :, 0, :], new_values[:, :, 0, :], suffix_lengths, group_size, scale,
    )
    parts = prefix_parts(gathered, keys, values, other_keys, other_values, group, scale)
    parts = lax.all_to_all(parts, "seq", 0, 0, axis_index_groups=same_core, tiled=True)
    attended = combine(
        parts, mean.reshape(group, head_dim), top.reshape(group, head_dim),
        total.reshape(group, head_dim), owned * steps,
    )
    attended = lax.all_to_all(
        jnp.tile(attended, (sharers, 1)), "seq", 0, 0, axis_index_groups=same_core, tiled=True
    )
    other_attended = lax.ppermute(attended, "seq", swap_cores)
    core = lax.axis_index("seq") % 2
    even = jnp.where(core == 0, attended, other_attended)
    odd = jnp.where(core == 0, other_attended, attended)
    attended = jnp.stack(
        [rows.reshape(sharers, owned * steps, row_width) for rows in (even, odd)], axis=1
    ).reshape(everyone * steps, row_width)
    partial = jnp.dot(attended, out_weight, preferred_element_type=jnp.float32)
    columns = out_weight.shape[1]
    heads = lax.axis_size("head")
    partial = partial.astype(jnp.bfloat16).reshape(heads, everyone * steps // heads, columns)
    partial = lax.all_to_all(partial, "head", 0, 0, tiled=True)
    summed = jnp.sum(partial.astype(jnp.float32), axis=0).astype(jnp.bfloat16)
    return summed.reshape(everyone // heads, steps, columns)


def solution(mesh):
    placed = (
        P("seq", None, "head"),
        P("seq", "head", None),
        P("seq", "head", None),
        P("seq", None, "head", None),
        P("seq", None, "head", None),
        P("seq", None, "head", None),
        P("seq", None, "head", None),
        P("seq"),
        P("head", "seq"),
    )
    return jax.shard_map(
        shards, mesh=mesh, in_specs=placed, out_specs=P("head", None, "seq"), check_vma=False
    )
```

profile of v0, /device:TPU:1, one launch (start us, length us, event | category | flops | bytes accessed | tf_op | source)
XLA Modules:
  0.0 109.0 jit_solution(5241344847026267553)
XLA Ops:
  0.0 0.0 copy-start
  0.0 3.2 %collective-permute-start = (bf16[4096,128]{1,0:T(8,128)(2,1)}, bf16[4096,128]{1,0:T(8,128)(2,1)S(1)}, u32[]{:S(2)}, u32[]{:S(2)}) collective-permute-start(bf16[4096,128]{1,0:T(8,128)(2,1)} %bitcast.30), channel_id=1, source_target_pairs={{0,8},{8,0},{16,24},{24,16},{32,40},{40,32},{48,56},{56,48},{64,72... | collective-permute-start | bytes 3145736 | tf_op jit(solution)/shard_map/ppermute | solution.py:345
  3.2 0.0 collective-permute-start.1
  3.2 0.7 reshape.38
  4.0 21.3 %all_to_all.27 = bf16[16,64,128]{2,1,0:T(8,128)(2,1)S(1)} all-to-all(bf16[16,64,128]{2,1,0:T(8,128)(2,1)S(1)} %tile.4), channel_id=1, replica_groups={{0,16,32,48,64,80,96,112,128,144,160,176,192,208,224,240},{8,24,40,56,7..., dimensions={0} | all-to-all | bytes 524288 | tf_op jit(solution)/shard_map/all_to_all | solution.py:342
  25.4 0.0 collective-permute-done.key_ref.other_key_ref
  25.4 0.0 collective-permute-done.1.value_ref.other_value_ref
  25.4 0.0 copy-start.4
  25.4 0.0 copy-start.5
  25.4 4.9 %prefix_first.1 = (f32[1024,128]{1,0:T(8,128)S(1)}, f32[1024,256]{1,0:T(8,128)S(1)}) custom-call(bf16[1024,128]{1,0:T(8,128)(2,1)S(1)} %bitcast.22, bf16[4096,128]{1,0:T(8,128)(2,1)S(1)} %collective-permute-done.key_ref.other_key_ref, bf16[4096,128]{1,0:T(8,128)(2,1)S(1)} %collective-permute-done.1.value_ref.other_value_ref), custom_call_target="tpu_custom_call" | custom-call | flops 3221225472 | bytes 2097152 | tf_op jit(solution)/shard_map/prefix_first/pallas_call | solution.py:139
  30.3 0.0 copy-done.4
  30.3 0.0 copy-done.5
  30.3 0.0 copy-start.1
  30.3 0.0 copy-start.2
  30.4 0.0 copy-start.3
  30.4 5.8 %prefix_second.1 = bf16[16,80,128]{2,1,0:T(8,128)(2,1)} custom-call(bf16[1024,128]{1,0:T(8,128)(2,1)S(1)} %bitcast.23, bf16[4096,128]{1,0:T(8,128)(2,1)S(1)} %bitcast.31, bf16[4096,128]{1,0:T(8,128)(2,1)S(1)} %bitcast.33, bf16[4096,128]{1,0:T(8,128)(2,1)S(1)} %collective-permute-done.key_ref.other_key_ref, ...), custom_call_target="tpu_custom_call" | custom-call | flops 3221225472 | bytes 2097152 | tf_op jit(solution)/shard_map/prefix_second/pallas_call | solution.py:151
  36.2 29.4 %all-to-all-start.1 = ((bf16[16,80,128]{2,1,0:T(8,128)(2,1)}), bf16[16,80,128]{2,1,0:T(8,128)(2,1)S(1)}, u32[]{:S(2)}, u32[]{:S(2)}) async-start(bf16[16,80,128]{2,1,0:T(8,128)(2,1)} %prefix_second.1), calls=%async_computation.1 | async-start | bytes 655360 | tf_op jit(solution)/shard_map/all_to_all | solution.py:353
  65.6 0.0 copy-done.1
  65.7 0.0 copy-done.2
  65.7 0.0 copy-done.3
  65.7 6.7 %suffix_part.1 = (f32[4,16,128]{2,1,0:T(8,128)S(1)}, f32[4,16,128]{2,1,0:T(8,128)S(1)}, f32[4,16,128]{2,1,0:T(8,128)S(1)}) custom-call(s32[4]{0:T(128)S(1)} %copy-done.3, bf16[4,16,128]{2,1,0:T(8,128)(2,1)S(1)} %bitcast.24, bf16[4,2,128]{2,1,0:T(2,128)(2,1)S(1)} %bitcast.28, bf16[4,2,128]{2,1,0:T(2,128)(2,1)S(1)} %bitcast.29, ...), custom_call_target="tpu_custom_call" | custom-call | flops 134217728 | bytes 8388608 | tf_op jit(solution)/shard_map/suffix_part/pallas_call | solution.py:271
  72.4 5.7 %all-to-all-done.1.part_ref = bf16[16,80,128]{2,1,0:T(8,128)(2,1)S(1)} async-done(((bf16[16,80,128]{2,1,0:T(8,128)(2,1)}), bf16[16,80,128]{2,1,0:T(8,128)(2,1)S(1)}, u32[]{:S(2)}, u32[]{:S(2)}) %all-to-all-start.1) | async-done | bytes 327712 | tf_op jit(solution)/shard_map/all_to_all | solution.py:353
  78.1 0.7 combine_parts.1
  78.7 15.0 %all_to_all.28 = bf16[16,8,1024]{2,1,0:T(8,128)(2,1)S(1)} all-to-all(bf16[16,8,1024]{2,1,0:T(8,128)(2,1)S(1)} %tile.5), channel_id=1, replica_groups={{0,16,32,48,64,80,96,112,128,144,160,176,192,208,224,240},{8,24,40,56,7..., dimensions={0} | all-to-all | bytes 524288 | tf_op jit(solution)/shard_map/all_to_all | solution.py:358
  93.8 3.5 %collective-permute-start.2 = (bf16[128,1024]{1,0:T(8,128)(2,1)S(1)}, bf16[128,1024]{1,0:T(8,128)(2,1)S(1)}, u32[]{:S(2)}, u32[]{:S(2)}) collective-permute-start(bf16[128,1024]{1,0:T(8,128)(2,1)S(1)} %bitcast.37), channel_id=1, source_target_pairs={{0,8},{8,0},{16,24},{24,16},{32,40},{40,32},{48,56},{56,48},{64,72... | collective-permute-start | bytes 786440 | tf_op jit(solution)/shard_map/ppermute | solution.py:361
  97.3 1.2 %collective-permute-done.2 = bf16[128,1024]{1,0:T(8,128)(2,1)S(1)} collective-permute-done((bf16[128,1024]{1,0:T(8,128)(2,1)S(1)}, bf16[128,1024]{1,0:T(8,128)(2,1)S(1)}, u32[]{:S(2)}, u32[]{:S(2)}) %collective-permute-start.2) | collective-permute-done | bytes 262176 | tf_op jit(solution)/shard_map/ppermute | solution.py:361
  98.5 0.1 pad_maximum_fusion
  98.5 0.0 copy-done
  98.5 0.3 convolution_convert_fusion
  98.8 9.5 %all_to_all.29 = bf16[8,32,256]{2,1,0:T(8,128)(2,1)S(1)} all-to-all(bf16[8,32,256]{2,1,0:T(8,128)(2,1)S(1)} %bitcast.38), channel_id=1, replica_groups=mesh['seq'=32,'head'=8] {'head'}, dimensions={0} | all-to-all | bytes 262144 | tf_op jit(solution)/shard_map/all_to_all | solution.py:372
  108.4 0.6 reshape.45
  (4 shorter events, 0.1 us)
Async XLA Ops:
  0.0 98.5 %copy-start = (bf16[1024,256]{1,0:T(8,128)(2,1)S(1)}, bf16[1024,256]{1,0:T(8,128)(2,1)}, u32[]{:S(2)}) copy-start(bf16[1024,256]{1,0:T(8,128)(2,1)} %param.17) | copy-start | bytes 1572868
  0.0 25.4 %collective-permute-start = (bf16[4096,128]{1,0:T(8,128)(2,1)}, bf16[4096,128]{1,0:T(8,128)(2,1)S(1)}, u32[]{:S(2)}, u32[]{:S(2)}) collective-permute-start(bf16[4096,128]{1,0:T(8,128)(2,1)} %bitcast.30), channel_id=1, source_target_pairs={{0,8},{8,0},{16,24},{24,16},{32,40},{40,32},{48,56},{56,48},{64,72... | collective-permute-start | bytes 3145736 | tf_op jit(solution)/shard_map/ppermute | solution.py:345
  3.2 22.1 %collective-permute-start.1 = (bf16[4096,128]{1,0:T(8,128)(2,1)}, bf16[4096,128]{1,0:T(8,128)(2,1)S(1)}, u32[]{:S(2)}, u32[]{:S(2)}) collective-permute-start(bf16[4096,128]{1,0:T(8,128)(2,1)} %bitcast.32), channel_id=1, source_target_pairs={{0,8},{8,0},{16,24},{24,16},{32,40},{40,32},{48,56},{56,48},{64,72... | collective-permute-start | bytes 3145736 | tf_op jit(solution)/shard_map/ppermute | solution.py:346
  25.4 5.0 %copy-start.4 = (bf16[4096,1,128]{2,0,1:T(8,128)(2,1)S(1)}, bf16[4096,1,128]{2,0,1:T(8,128)(2,1)}, u32[]{:S(2)}) copy-start(bf16[4096,1,128]{2,0,1:T(8,128)(2,1)} %param.10) | copy-start | bytes 3145732
  25.4 5.0 %copy-start.5 = (bf16[4096,1,128]{2,0,1:T(8,128)(2,1)S(1)}, bf16[4096,1,128]{2,0,1:T(8,128)(2,1)}, u32[]{:S(2)}) copy-start(bf16[4096,1,128]{2,0,1:T(8,128)(2,1)} %param.11) | copy-start | bytes 3145732
  30.3 35.3 %copy-start.1 = (bf16[4,2,1,128]{3,1,2,0:T(2,128)(2,1)S(1)}, bf16[4,2,1,128]{3,1,2,0:T(2,128)(2,1)}, u32[]{:S(2)}) copy-start(bf16[4,2,1,128]{3,1,2,0:T(2,128)(2,1)} %param.14) | copy-start | bytes 6148
  30.3 35.3 %copy-start.2 = (bf16[4,2,1,128]{3,1,2,0:T(2,128)(2,1)S(1)}, bf16[4,2,1,128]{3,1,2,0:T(2,128)(2,1)}, u32[]{:S(2)}) copy-start(bf16[4,2,1,128]{3,1,2,0:T(2,128)(2,1)} %param.15) | copy-start | bytes 6148
  30.4 35.3 %copy-start.3 = (s32[4]{0:T(128)S(1)}, s32[4]{0:T(128)}, u32[]{:S(2)}) copy-start(s32[4]{0:T(128)} %length_ref.1) | copy-start | bytes 52
  36.2 41.9 %all-to-all-start.1 = ((bf16[16,80,128]{2,1,0:T(8,128)(2,1)}), bf16[16,80,128]{2,1,0:T(8,128)(2,1)S(1)}, u32[]{:S(2)}, u32[]{:S(2)}) async-start(bf16[16,80,128]{2,1,0:T(8,128)(2,1)} %prefix_second.1), calls=%async_computation.1 | async-start | bytes 655360 | tf_op jit(solution)/shard_map/all_to_all | solution.py:353
  93.8 4.7 %collective-permute-start.2 = (bf16[128,1024]{1,0:T(8,128)(2,1)S(1)}, bf16[128,1024]{1,0:T(8,128)(2,1)S(1)}, u32[]{:S(2)}, u32[]{:S(2)}) collective-permute-start(bf16[128,1024]{1,0:T(8,128)(2,1)S(1)} %bitcast.37), channel_id=1, source_target_pairs={{0,8},{8,0},{16,24},{24,16},{32,40},{40,32},{48,56},{56,48},{64,72... | collective-permute-start | bytes 786440 | tf_op jit(solution)/shard_map/ppermute | solution.py:361
where the time goes:
time: 109 us
  blocking collectives  45.8 us (42%)
  starting transfers between devices  36.2 us (33%)
  Pallas kernels  18.1 us (17%)
  waiting for transfers between devices  6.84 us (6%)
  local copies, waits for them, and re-layouts  1.46 us (1%)
    all_to_all x1, starting transfers between devices, shards(): lax.all_to_all(parts, 'seq', 0, 0, axis_index_groups=same_core, tiled=True)  29.4 us
    all_to_all x1, blocking collectives, shards(): lax.all_to_all(jnp.tile(own_rows, (sharers, 1)), 'seq', 0, 0, axis_index_...  21.3 us
    all_to_all x1, blocking collectives, shards(): lax.all_to_all(jnp.tile(attended, (sharers, 1)), 'seq', 0, 0, axis_index_...  15 us
    all_to_all x1, blocking collectives, shards(): partial = lax.all_to_all(partial, 'head', 0, 0, tiled=True)  9.5 us
    pallas_call x1, Pallas kernels, suffix_part(): pl.pallas_call(functools.partial(suffix_kernel, key_block=key_block, grou...  6.7 us
    pallas_call x1, Pallas kernels, prefix_parts(): pl.pallas_call(functools.partial(second_kernel, key_block=key_block, grou...  5.82 us
    all_to_all x1, waiting for transfers between devices, shards(): lax.all_to_all(parts, 'seq', 0, 0, axis_index_groups=same_core, tiled=True)  5.68 us
    pallas_call x1, Pallas kernels, prefix_parts(): pl.pallas_call(functools.partial(first_kernel, key_block=key_block, scale...  4.93 us
  transfers between devices with their start and end apart: 4, of which 2 were waited for; matrix products, arithmetic and copies ran while one was open for 1% of the time, Pallas kernels for 6%

commit v1 on v0

--- a/solution.py
+++ b/solution.py
@@ -78,51 +78,75 @@
     return top, acc
 
 
-def first_kernel(query_ref, key_ref, value_ref, top_ref, state_ref, *, key_block, scale):
-    top, acc = shifted_softmax(query_ref[...], key_ref, value_ref, key_block, scale, None, None)
-    top_ref[...] = jnp.broadcast_to(top, top_ref.shape)
-    state_ref[...] = acc
-
-
-def second_kernel(
-    query_ref, key_ref, value_ref, other_key_ref, other_value_ref, first_top_ref, state_ref, out_ref,
-    top_ref, total_ref, acc_ref, *, key_block, group, scale,
-):
-    query_rows = query_ref[...]
-    count, head_dim = query_rows.shape
-    top = first_top_ref[...]
-    wide = jnp.concatenate([top] * (key_block // head_dim), axis=1)
-    _, acc = shifted_softmax(
-        query_rows, key_ref, value_ref, key_block, scale, wide, state_ref[...]
-    )
-    total = acc[:, head_dim:]
-    top_ref[...] = top
-    total_ref[...] = total
-    acc_ref[...] = acc[:, :head_dim]
-
-    @pl.when(jnp.logical_not(jnp.max(total) < TOTAL_MAX))
-    def _():
-        top, total, acc = running_softmax(
-            query_rows, (other_key_ref, key_ref), (other_value_ref, value_ref), key_block, scale
+def first_kernel(query_ref, key_ref, value_ref, top_ref, state_ref, *, chunk, key_block, scale):
+    for start in range(0, query_ref.shape[0], chunk):
+        rows = slice(start, start + chunk)
+        top, acc = shifted_softmax(
+            query_ref[rows, :], key_ref, value_ref, key_block, scale, None, None
         )
-        top_ref[...] = jnp.broadcast_to(top, (count, head_dim))
-        total_ref[...] = jnp.broadcast_to(total, (count, head_dim))
-        acc_ref[...] = acc
-
+        top_ref[rows, :] = jnp.broadcast_to(top, (chunk, top_ref.shape[1]))
+        state_ref[rows, :] = acc
+
+
+def write_parts(out_ref, first, group, top, total, acc):
+    head_dim = acc.shape[1]
     row = lax.broadcasted_iota(jnp.int32, (group, head_dim), 0)
     lane = lax.broadcasted_iota(jnp.int32, (group, head_dim), 1)
     tile_row = lax.broadcasted_iota(jnp.int32, (STAT_ROWS, head_dim), 0)
-    for index in range(count // group):
+    for index in range(acc.shape[0] // group):
         rows = slice(index * group, (index + 1) * group)
-        total = total_ref[rows, :]
-        stat = jnp.where(lane == row, top_ref[rows, :], 0.0)
-        stat = jnp.where(lane == row + group, total, stat)
+        stat = jnp.where(lane == row, top[rows], 0.0)
+        stat = jnp.where(lane == row + group, total[rows], stat)
         high, middle, low = split_bf16(jnp.sum(stat, axis=0, keepdims=True))
-        out_ref[index, :group, :] = (acc_ref[rows, :] / total).astype(jnp.bfloat16)
+        out_ref[first + index, :group, :] = (acc[rows] / total[rows]).astype(jnp.bfloat16)
         tile = jnp.where(tile_row == 0, high.astype(jnp.float32), 0.0)
         tile = jnp.where(tile_row == 1, middle.astype(jnp.float32), tile)
         tile = jnp.where(tile_row == 2, low.astype(jnp.float32), tile)
-        out_ref[index, group:, :] = tile.astype(jnp.bfloat16)
+        out_ref[first + index, group:, :] = tile.astype(jnp.bfloat16)
+
+
+def second_kernel(
+    query_ref, key_ref, value_ref, other_key_ref, other_value_ref, top_ref, state_ref, out_ref,
+    part_ref, sems, *, chunk, key_block, group, scale,
+):
+    count, head_dim = query_ref.shape
+    owners = chunk // group
+    copies = []
+    largest = None
+    for start in range(0, count, chunk):
+        rows = slice(start, start + chunk)
+        top = top_ref[rows, :]
+        wide = jnp.concatenate([top] * (key_block // head_dim), axis=1)
+        _, acc = shifted_softmax(
+            query_ref[rows, :], key_ref, value_ref, key_block, scale, wide, state_ref[rows, :]
+        )
+        total = acc[:, head_dim:]
+        largest = total if largest is None else jnp.maximum(largest, total)
+        write_parts(part_ref, start // group, group, top, total, acc[:, :head_dim])
+        span = pl.ds(start // group, owners)
+        copy = pltpu.make_async_copy(part_ref.at[span], out_ref.at[span], sems.at[start // chunk])
+        copy.start()
+        copies.append(copy)
+    for copy in copies:
+        copy.wait()
+
+    @pl.when(jnp.logical_not(jnp.max(largest) < TOTAL_MAX))
+    def _():
+        for start in range(0, count, chunk):
+            rows = slice(start, start + chunk)
+            top, total, acc = running_softmax(
+                query_ref[rows, :],
+                (other_key_ref, key_ref),
+                (other_value_ref, value_ref),
+                key_block,
+                scale,
+            )
+            wide = (chunk, head_dim)
+            top, total = jnp.broadcast_to(top, wide), jnp.broadcast_to(total, wide)
+            write_parts(part_ref, start // group, group, top, total, acc)
+        copy = pltpu.make_async_copy(part_ref, out_ref, sems.at[0])
+        copy.start()
+        copy.wait()
 
 
 def prefix_parts(query_rows, keys, values, other_keys, other_values, group, scale):
@@ -131,13 +155,14 @@
     held = pl.BlockSpec(memory_space=pltpu.VMEM)
     limit = pltpu.CompilerParams(vmem_limit_bytes=32 * 2**20)
     key_block = min(256, positions)
+    chunk = min(256, count)
     cost = pl.CostEstimate(
         flops=6 * count * positions * head_dim,
         bytes_accessed=4 * positions * head_dim,
         transcendentals=count * positions,
     )
     top, state = pl.pallas_call(
-        functools.partial(first_kernel, key_block=key_block, scale=scale),
+        functools.partial(first_kernel, chunk=chunk, key_block=key_block, scale=scale),
         in_specs=[held] * 3,
         out_specs=[held] * 2,
         out_shape=[
@@ -148,14 +173,18 @@
         cost_estimate=cost,
         name="prefix_first",
     )(query_rows, other_keys, other_values)
+    shape = (count // group, group + STAT_ROWS, head_dim)
     return pl.pallas_call(
-        functools.partial(second_kernel, key_block=key_block, group=group, scale=scale),
+        functools.partial(
+            second_kernel, chunk=chunk, key_block=key_block, group=group, scale=scale
+        ),
         in_specs=[held] * 7,
-        out_specs=held,
-        out_shape=jax.ShapeDtypeStruct(
-            (count // group, group + STAT_ROWS, head_dim), jnp.bfloat16
-        ),
-        scratch_shapes=[pltpu.VMEM((count, head_dim), jnp.float32)] * 3,
+        out_specs=pl.BlockSpec(memory_space=pltpu.HBM),
+        out_shape=jax.ShapeDtypeStruct(shape, jnp.bfloat16),
+        scratch_shapes=[
+            pltpu.VMEM(shape, jnp.bfloat16),
+            pltpu.SemaphoreType.DMA((count // chunk,)),
+        ],
         compiler_params=limit,
         cost_estimate=cost,
         name="prefix_second",

time: 109 us -> 140 us (1.28)
  starting transfers between devices: 36.2 us -> 67.2 us
  Pallas kernels: 18.1 us -> 16.7 us
    all_to_all x1, starting transfers between devices: 29.4 us -> 60.4 us  [shards(): lax.all_to_all(parts, 'seq', 0, 0, axis_index_groups=same_core, tiled=True)]
  transfers between devices with their start and end apart: 4 -> 4, of which waited for: 2 -> 2; matrix products, arithmetic and copies ran while one was open for 1% -> 1% of each run, Pallas kernels for 6% -> 4%
where the time goes in v1:
time: 140 us
  starting transfers between devices  67.2 us (48%)
  blocking collectives  45.9 us (33%)
  Pallas kernels  16.7 us (12%)
  waiting for transfers between devices  7.9 us (6%)
  local copies, waits for them, and re-layouts  1.46 us (1%)
    all_to_all x1, starting transfers between devices, shards(): lax.all_to_all(parts, 'seq', 0, 0, axis_index_groups=same_core, tiled=True)  60.4 us
    all_to_all x1, blocking collectives, shards(): lax.all_to_all(jnp.tile(own_rows, (sharers, 1)), 'seq', 0, 0, axis_index_...  21.3 us
    all_to_all x1, blocking collectives, shards(): lax.all_to_all(jnp.tile(attended, (sharers, 1)), 'seq', 0, 0, axis_index_...  15 us
    all_to_all x1, blocking collectives, shards(): partial = lax.all_to_all(partial, 'head', 0, 0, tiled=True)  9.5 us
    all_to_all x1, waiting for transfers between devices, shards(): lax.all_to_all(parts, 'seq', 0, 0, axis_index_groups=same_core, tiled=True)  6.73 us
    pallas_call x1, Pallas kernels, prefix_parts(): pl.pallas_call(functools.partial(second_kernel, chunk=chunk, key_block=ke...  5.66 us
    pallas_call x1, Pallas kernels, suffix_part(): pl.pallas_call(functools.partial(suffix_kernel, key_block=key_block, grou...  5.64 us
    pallas_call x1, Pallas kernels, prefix_parts(): pl.pallas_call(functools.partial(first_kernel, chunk=chunk, key_block=key...  4.8 us
  transfers between devices with their start and end apart: 4, of which 2 were waited for; matrix products, arithmetic and copies ran while one was open for 1% of the time, Pallas kernels for 4%

profile of v1, /device:TPU:1, one launch (start us, length us, event | category | flops | bytes accessed | tf_op | source)
XLA Modules:
  0.0 139.7 jit_solution(6613231886748096486)
XLA Ops:
  0.0 0.0 copy-start
  0.0 3.2 %collective-permute-start = (bf16[4096,128]{1,0:T(8,128)(2,1)}, bf16[4096,128]{1,0:T(8,128)(2,1)S(1)}, u32[]{:S(2)}, u32[]{:S(2)}) collective-permute-start(bf16[4096,128]{1,0:T(8,128)(2,1)} %bitcast.30), channel_id=1, source_target_pairs={{0,8},{8,0},{16,24},{24,16},{32,40},{40,32},{48,56},{56,48},{64,72... | collective-permute-start | bytes 3145736 | tf_op jit(solution)/shard_map/ppermute | solution.py:374
  3.2 0.0 collective-permute-start.1
  3.2 0.7 reshape.38
  4.0 21.3 %all_to_all.27 = bf16[16,64,128]{2,1,0:T(8,128)(2,1)S(1)} all-to-all(bf16[16,64,128]{2,1,0:T(8,128)(2,1)S(1)} %tile.4), channel_id=1, replica_groups={{0,16,32,48,64,80,96,112,128,144,160,176,192,208,224,240},{8,24,40,56,7..., dimensions={0} | all-to-all | bytes 524288 | tf_op jit(solution)/shard_map/all_to_all | solution.py:371
  25.4 0.0 collective-permute-done.key_ref.other_key_ref
  25.4 0.0 collective-permute-done.1.value_ref.other_value_ref
  25.4 0.0 copy-start.4
  25.4 0.0 copy-start.5
  25.4 4.8 %prefix_first.1 = (f32[1024,128]{1,0:T(8,128)S(1)}, f32[1024,256]{1,0:T(8,128)S(1)}) custom-call(bf16[1024,128]{1,0:T(8,128)(2,1)S(1)} %bitcast.22, bf16[4096,128]{1,0:T(8,128)(2,1)S(1)} %collective-permute-done.key_ref.other_key_ref, bf16[4096,128]{1,0:T(8,128)(2,1)S(1)} %collective-permute-done.1.value_ref.other_value_ref), custom_call_target="tpu_custom_call" | custom-call | flops 3221225472 | bytes 2097152 | tf_op jit(solution)/shard_map/prefix_first/pallas_call | solution.py:164
  30.2 0.0 copy-done.4
  30.2 0.0 copy-done.5
  30.2 0.0 copy-start.1
  30.2 0.0 copy-start.2
  30.2 0.0 copy-start.3
  30.2 5.7 %prefix_second.1 = bf16[16,80,128]{2,1,0:T(8,128)(2,1)} custom-call(bf16[1024,128]{1,0:T(8,128)(2,1)S(1)} %bitcast.23, bf16[4096,128]{1,0:T(8,128)(2,1)S(1)} %bitcast.31, bf16[4096,128]{1,0:T(8,128)(2,1)S(1)} %bitcast.33, bf16[4096,128]{1,0:T(8,128)(2,1)S(1)} %collective-permute-done.key_ref.other_key_ref, ...), custom_call_target="tpu_custom_call" | custom-call | flops 3221225472 | bytes 2097152 | tf_op jit(solution)/shard_map/prefix_second/pallas_call | solution.py:177
  35.9 60.4 %all-to-all-start.1 = ((bf16[16,80,128]{2,1,0:T(8,128)(2,1)}), bf16[16,80,128]{2,1,0:T(8,128)(2,1)S(1)}, u32[]{:S(2)}, u32[]{:S(2)}) async-start(bf16[16,80,128]{2,1,0:T(8,128)(2,1)} %prefix_second.1), calls=%async_computation.1 | async-start | bytes 655360 | tf_op jit(solution)/shard_map/all_to_all | solution.py:382
  96.3 0.0 copy-done.1
  96.3 0.0 copy-done.2
  96.4 0.0 copy-done.3
  96.4 5.6 %suffix_part.1 = (f32[4,16,128]{2,1,0:T(8,128)S(1)}, f32[4,16,128]{2,1,0:T(8,128)S(1)}, f32[4,16,128]{2,1,0:T(8,128)S(1)}) custom-call(s32[4]{0:T(128)S(1)} %copy-done.3, bf16[4,16,128]{2,1,0:T(8,128)(2,1)S(1)} %bitcast.24, bf16[4,2,128]{2,1,0:T(2,128)(2,1)S(1)} %bitcast.28, bf16[4,2,128]{2,1,0:T(2,128)(2,1)S(1)} %bitcast.29, ...), custom_call_target="tpu_custom_call" | custom-call | flops 134217728 | bytes 8388608 | tf_op jit(solution)/shard_map/suffix_part/pallas_call | solution.py:300
  102.0 6.7 %all-to-all-done.1.part_ref = bf16[16,80,128]{2,1,0:T(8,128)(2,1)S(1)} async-done(((bf16[16,80,128]{2,1,0:T(8,128)(2,1)}), bf16[16,80,128]{2,1,0:T(8,128)(2,1)S(1)}, u32[]{:S(2)}, u32[]{:S(2)}) %all-to-all-start.1) | async-done | bytes 327712 | tf_op jit(solution)/shard_map/all_to_all | solution.py:382
  108.7 0.7 combine_parts.1
  109.4 15.0 %all_to_all.28 = bf16[16,8,1024]{2,1,0:T(8,128)(2,1)S(1)} all-to-all(bf16[16,8,1024]{2,1,0:T(8,128)(2,1)S(1)} %tile.5), channel_id=1, replica_groups={{0,16,32,48,64,80,96,112,128,144,160,176,192,208,224,240},{8,24,40,56,7..., dimensions={0} | all-to-all | bytes 524288 | tf_op jit(solution)/shard_map/all_to_all | solution.py:387
  124.5 3.5 %collective-permute-start.2 = (bf16[128,1024]{1,0:T(8,128)(2,1)S(1)}, bf16[128,1024]{1,0:T(8,128)(2,1)S(1)}, u32[]{:S(2)}, u32[]{:S(2)}) collective-permute-start(bf16[128,1024]{1,0:T(8,128)(2,1)S(1)} %bitcast.37), channel_id=1, source_target_pairs={{0,8},{8,0},{16,24},{24,16},{32,40},{40,32},{48,56},{56,48},{64,72... | collective-permute-start | bytes 786440 | tf_op jit(solution)/shard_map/ppermute | solution.py:390
  128.0 1.2 collective-permute-done.2
  129.2 0.1 pad_maximum_fusion
  129.2 0.0 copy-done
  129.2 0.3 convolution_convert_fusion
  129.5 9.5 %all_to_all.29 = bf16[8,32,256]{2,1,0:T(8,128)(2,1)S(1)} all-to-all(bf16[8,32,256]{2,1,0:T(8,128)(2,1)S(1)} %bitcast.38), channel_id=1, replica_groups=mesh['seq'=32,'head'=8] {'head'}, dimensions={0} | all-to-all | bytes 262144 | tf_op jit(solution)/shard_map/all_to_all | solution.py:401
  139.1 0.6 reshape.45
  (4 shorter events, 0.1 us)
Async XLA Ops:
  0.0 129.2 %copy-start = (bf16[1024,256]{1,0:T(8,128)(2,1)S(1)}, bf16[1024,256]{1,0:T(8,128)(2,1)}, u32[]{:S(2)}) copy-start(bf16[1024,256]{1,0:T(8,128)(2,1)} %param.17) | copy-start | bytes 1572868
  0.0 25.4 %collective-permute-start = (bf16[4096,128]{1,0:T(8,128)(2,1)}, bf16[4096,128]{1,0:T(8,128)(2,1)S(1)}, u32[]{:S(2)}, u32[]{:S(2)}) collective-permute-start(bf16[4096,128]{1,0:T(8,128)(2,1)} %bitcast.30), channel_id=1, source_target_pairs={{0,8},{8,0},{16,24},{24,16},{32,40},{40,32},{48,56},{56,48},{64,72... | collective-permute-start | bytes 3145736 | tf_op jit(solution)/shard_map/ppermute | solution.py:374
  3.2 22.1 %collective-permute-start.1 = (bf16[4096,128]{1,0:T(8,128)(2,1)}, bf16[4096,128]{1,0:T(8,128)(2,1)S(1)}, u32[]{:S(2)}, u32[]{:S(2)}) collective-permute-start(bf16[4096,128]{1,0:T(8,128)(2,1)} %bitcast.32), channel_id=1, source_target_pairs={{0,8},{8,0},{16,24},{24,16},{32,40},{40,32},{48,56},{56,48},{64,72... | collective-permute-start | bytes 3145736 | tf_op jit(solution)/shard_map/ppermute | solution.py:375
  25.4 4.8 %copy-start.4 = (bf16[4096,1,128]{2,0,1:T(8,128)(2,1)S(1)}, bf16[4096,1,128]{2,0,1:T(8,128)(2,1)}, u32[]{:S(2)}) copy-start(bf16[4096,1,128]{2,0,1:T(8,128)(2,1)} %param.10) | copy-start | bytes 3145732
  25.4 4.8 %copy-start.5 = (bf16[4096,1,128]{2,0,1:T(8,128)(2,1)S(1)}, bf16[4096,1,128]{2,0,1:T(8,128)(2,1)}, u32[]{:S(2)}) copy-start(bf16[4096,1,128]{2,0,1:T(8,128)(2,1)} %param.11) | copy-start | bytes 3145732
  30.2 66.1 %copy-start.1 = (bf16[4,2,1,128]{3,1,2,0:T(2,128)(2,1)S(1)}, bf16[4,2,1,128]{3,1,2,0:T(2,128)(2,1)}, u32[]{:S(2)}) copy-start(bf16[4,2,1,128]{3,1,2,0:T(2,128)(2,1)} %param.14) | copy-start | bytes 6148
  30.2 66.1 %copy-start.2 = (bf16[4,2,1,128]{3,1,2,0:T(2,128)(2,1)S(1)}, bf16[4,2,1,128]{3,1,2,0:T(2,128)(2,1)}, u32[]{:S(2)}) copy-start(bf16[4,2,1,128]{3,1,2,0:T(2,128)(2,1)} %param.15) | copy-start | bytes 6148
  30.2 66.1 %copy-start.3 = (s32[4]{0:T(128)S(1)}, s32[4]{0:T(128)}, u32[]{:S(2)}) copy-start(s32[4]{0:T(128)} %length_ref.1) | copy-start | bytes 52
  35.9 72.8 %all-to-all-start.1 = ((bf16[16,80,128]{2,1,0:T(8,128)(2,1)}), bf16[16,80,128]{2,1,0:T(8,128)(2,1)S(1)}, u32[]{:S(2)}, u32[]{:S(2)}) async-start(bf16[16,80,128]{2,1,0:T(8,128)(2,1)} %prefix_second.1), calls=%async_computation.1 | async-start | bytes 655360 | tf_op jit(solution)/shard_map/all_to_all | solution.py:382
  124.5 4.7 %collective-permute-start.2 = (bf16[128,1024]{1,0:T(8,128)(2,1)S(1)}, bf16[128,1024]{1,0:T(8,128)(2,1)S(1)}, u32[]{:S(2)}, u32[]{:S(2)}) collective-permute-start(bf16[128,1024]{1,0:T(8,128)(2,1)S(1)} %bitcast.37), channel_id=1, source_target_pairs={{0,8},{8,0},{16,24},{24,16},{32,40},{40,32},{48,56},{56,48},{64,72... | collective-permute-start | bytes 786440 | tf_op jit(solution)/shard_map/ppermute | solution.py:390

commit v2 on v1

--- a/solution.py
+++ b/solution.py
@@ -10,6 +10,7 @@
 LOW = -1.0e30
 LOG2E = 1.4426950408889634
 STAT_ROWS = 16
+ONES_ROWS = 16
 TOTAL_MAX = 2.0**100
 
 
@@ -59,50 +60,69 @@
 
 
 def shifted_softmax(query_rows, key_ref, value_ref, key_block, scale, top, acc):
-    ones = jnp.ones((key_block, query_rows.shape[1]), jnp.bfloat16)
+    ones = jnp.ones((ONES_ROWS, key_block), jnp.bfloat16)
     spans = [slice(start, start + key_block) for start in range(0, key_ref.shape[0], key_block)]
 
     def score(span):
-        return dot_rows(query_rows, key_ref[span, :]) * scale
+        return dot_rows(key_ref[span, :], query_rows) * scale
 
     scores = score(spans[0])
     for index, span in enumerate(spans):
         later = score(spans[index + 1]) if index + 1 < len(spans) else None
         if top is None:
-            top = jnp.max(scores, axis=1, keepdims=True)
+            top = jnp.max(scores, axis=0, keepdims=True)
         weights = jnp.exp2(scores - top).astype(jnp.bfloat16)
-        values = jnp.concatenate([value_ref[span, :], ones], axis=1)
-        part = jnp.dot(weights, values, preferred_element_type=jnp.float32)
+        values = jnp.concatenate([value_ref[span, :].T, ones], axis=0)
+        part = jnp.dot(values, weights, preferred_element_type=jnp.float32)
         acc = part if acc is None else acc + part
         scores = later
     return top, acc
 
 
-def first_kernel(query_ref, key_ref, value_ref, top_ref, state_ref, *, chunk, key_block, scale):
-    for start in range(0, query_ref.shape[0], chunk):
-        rows = slice(start, start + chunk)
-        top, acc = shifted_softmax(
-            query_ref[rows, :], key_ref, value_ref, key_block, scale, None, None
+def first_kernel(query_ref, key_ref, value_ref, top_ref, state_ref, *, key_block, scale):
+    top_ref[...], state_ref[...] = shifted_softmax(
+        query_ref[...], key_ref, value_ref, key_block, scale, None, None
+    )
+
+
+def stat_tile(stat):
+    high, middle, low = split_bf16(stat)
+    row = lax.broadcasted_iota(jnp.int32, stat.shape, 0)
+    tile = jnp.where(row == 0, high.astype(jnp.float32), 0.0)
+    tile = jnp.where(row == 1, middle.astype(jnp.float32), tile)
+    tile = jnp.where(row == 2, low.astype(jnp.float32), tile)
+    return tile.astype(jnp.bfloat16)
+
+
+def write_columns(out_ref, first, group, top, total, acc):
+    head_dim = acc.shape[0]
+    lane = lax.broadcasted_iota(jnp.int32, (STAT_ROWS, head_dim), 1)
+    for index in range(acc.shape[1] // head_dim):
+        lanes = slice(index * head_dim, (index + 1) * head_dim)
+        mean = (acc[:, lanes] / total[:, lanes]).T.astype(jnp.bfloat16)
+        tops = jnp.broadcast_to(top[:, lanes], (STAT_ROWS, head_dim))
+        totals = jnp.broadcast_to(total[:, lanes], (STAT_ROWS, head_dim))
+        stats = (
+            jnp.where(lane < group, tops, pltpu.roll(totals, group, 1)),
+            jnp.where(lane < group, pltpu.roll(tops, group, 1), totals),
         )
-        top_ref[rows, :] = jnp.broadcast_to(top, (chunk, top_ref.shape[1]))
-        state_ref[rows, :] = acc
+        for side, stat in enumerate(stats):
+            place = first + 2 * index + side
+            out_ref[place, :group, :] = mean[side * group : (side + 1) * group]
+            out_ref[place, group:, :] = stat_tile(stat)
 
 
 def write_parts(out_ref, first, group, top, total, acc):
     head_dim = acc.shape[1]
     row = lax.broadcasted_iota(jnp.int32, (group, head_dim), 0)
     lane = lax.broadcasted_iota(jnp.int32, (group, head_dim), 1)
-    tile_row = lax.broadcasted_iota(jnp.int32, (STAT_ROWS, head_dim), 0)
     for index in range(acc.shape[0] // group):
         rows = slice(index * group, (index + 1) * group)
         stat = jnp.where(lane == row, top[rows], 0.0)
         stat = jnp.where(lane == row + group, total[rows], stat)
-        high, middle, low = split_bf16(jnp.sum(stat, axis=0, keepdims=True))
+        stat = jnp.broadcast_to(jnp.sum(stat, axis=0, keepdims=True), (STAT_ROWS, head_dim))
         out_ref[first + index, :group, :] = (acc[rows] / total[rows]).astype(jnp.bfloat16)
-        tile = jnp.where(tile_row == 0, high.astype(jnp.float32), 0.0)
-        tile = jnp.where(tile_row == 1, middle.astype(jnp.float32), tile)
-        tile = jnp.where(tile_row == 2, low.astype(jnp.float32), tile)
-        out_ref[first + index, group:, :] = tile.astype(jnp.bfloat16)
+        out_ref[first + index, group:, :] = stat_tile(stat)
 
 
 def second_kernel(
@@ -112,17 +132,16 @@
     count, head_dim = query_ref.shape
     owners = chunk // group
     copies = []
-    largest = None
+    top = top_ref[...]
+    _, acc = shifted_softmax(
+        query_ref[...], key_ref, value_ref, key_block, scale, top, state_ref[...]
+    )
+    totals = acc[head_dim : head_dim + 1]
     for start in range(0, count, chunk):
-        rows = slice(start, start + chunk)
-        top = top_ref[rows, :]
-        wide = jnp.concatenate([top] * (key_block // head_dim), axis=1)
-        _, acc = shifted_softmax(
-            query_ref[rows, :], key_ref, value_ref, key_block, scale, wide, state_ref[rows, :]
+        lanes = slice(start, start + chunk)
+        write_columns(
+            part_ref, start // group, group, top[:, lanes], totals[:, lanes], acc[:head_dim, lanes]
         )
-        total = acc[:, head_dim:]
-        largest = total if largest is None else jnp.maximum(largest, total)
-        write_parts(part_ref, start // group, group, top, total, acc[:, :head_dim])
         span = pl.ds(start // group, owners)
         copy = pltpu.make_async_copy(part_ref.at[span], out_ref.at[span], sems.at[start // chunk])
         copy.start()
@@ -130,7 +149,7 @@
     for copy in copies:
         copy.wait()
 
-    @pl.when(jnp.logical_not(jnp.max(largest) < TOTAL_MAX))
+    @pl.when(jnp.logical_not(jnp.max(totals) < TOTAL_MAX))
     def _():
         for start in range(0, count, chunk):
             rows = slice(start, start + chunk)
@@ -162,12 +181,12 @@
         transcendentals=count * positions,
     )
     top, state = pl.pallas_call(
-        functools.partial(first_kernel, chunk=chunk, key_block=key_block, scale=scale),
+        functools.partial(first_kernel, key_block=key_block, scale=scale),
         in_specs=[held] * 3,
         out_specs=[held] * 2,
         out_shape=[
-            jax.ShapeDtypeStruct((count, head_dim), jnp.float32),
-            jax.ShapeDtypeStruct((count, 2 * head_dim), jnp.float32),
+            jax.ShapeDtypeStruct((1, count), jnp.float32),
+            jax.ShapeDtypeStruct((head_dim + ONES_ROWS, count), jnp.float32),
         ],
         compiler_params=limit,
         cost_estimate=cost,

time: 140 us -> 138 us (0.986)
  transfers between devices with their start and end apart: 4 -> 4, of which waited for: 2 -> 2; matrix products, arithmetic and copies ran while one was open for 1% -> 1% of each run, Pallas kernels for 4% -> 5%
where the time goes in v2:
time: 138 us
  starting transfers between devices  67.2 us (49%)
  blocking collectives  45.9 us (33%)
  Pallas kernels  16 us (12%)
  waiting for transfers between devices  6.83 us (5%)
  local copies, waits for them, and re-layouts  1.46 us (1%)
    all_to_all x1, starting transfers between devices, shards(): lax.all_to_all(parts, 'seq', 0, 0, axis_index_groups=same_core, tiled=True)  60.4 us
    all_to_all x1, blocking collectives, shards(): lax.all_to_all(jnp.tile(own_rows, (sharers, 1)), 'seq', 0, 0, axis_index_...  21.3 us
    all_to_all x1, blocking collectives, shards(): lax.all_to_all(jnp.tile(attended, (sharers, 1)), 'seq', 0, 0, axis_index_...  15 us
    all_to_all x1, blocking collectives, shards(): partial = lax.all_to_all(partial, 'head', 0, 0, tiled=True)  9.51 us
    pallas_call x1, Pallas kernels, suffix_part(): pl.pallas_call(functools.partial(suffix_kernel, key_block=key_block, grou...  6.7 us
    all_to_all x1, waiting for transfers between devices, shards(): lax.all_to_all(parts, 'seq', 0, 0, axis_index_groups=same_core, tiled=True)  5.66 us
    pallas_call x1, Pallas kernels, prefix_parts(): pl.pallas_call(functools.partial(second_kernel, chunk=chunk, key_block=ke...  4.64 us
    pallas_call x1, Pallas kernels, prefix_parts(): pl.pallas_call(functools.partial(first_kernel, key_block=key_block, scale...  4.01 us
  transfers between devices with their start and end apart: 4, of which 2 were waited for; matrix products, arithmetic and copies ran while one was open for 1% of the time, Pallas kernels for 5%

profile of v2, /device:TPU:1, one launch (start us, length us, event | category | flops | bytes accessed | tf_op | source)
XLA Modules:
  0.0 137.9 jit_solution(17191427147972469418)
XLA Ops:
  0.0 0.0 copy-start
  0.0 3.2 %collective-permute-start = (bf16[4096,128]{1,0:T(8,128)(2,1)}, bf16[4096,128]{1,0:T(8,128)(2,1)S(1)}, u32[]{:S(2)}, u32[]{:S(2)}) collective-permute-start(bf16[4096,128]{1,0:T(8,128)(2,1)} %bitcast.30), channel_id=1, source_target_pairs={{0,8},{8,0},{16,24},{24,16},{32,40},{40,32},{48,56},{56,48},{64,72... | collective-permute-start | bytes 3145736 | tf_op jit(solution)/shard_map/ppermute | solution.py:393
  3.2 0.0 collective-permute-start.1
  3.2 0.7 reshape.38
  4.0 21.3 %all_to_all.27 = bf16[16,64,128]{2,1,0:T(8,128)(2,1)S(1)} all-to-all(bf16[16,64,128]{2,1,0:T(8,128)(2,1)S(1)} %tile.4), channel_id=1, replica_groups={{0,16,32,48,64,80,96,112,128,144,160,176,192,208,224,240},{8,24,40,56,7..., dimensions={0} | all-to-all | bytes 524288 | tf_op jit(solution)/shard_map/all_to_all | solution.py:390
  25.4 0.0 collective-permute-done.key_ref.other_key_ref
  25.4 0.0 collective-permute-done.1.value_ref.other_value_ref
  25.4 0.0 copy-start.4
  25.4 0.0 copy-start.5
  25.4 4.0 %prefix_first.1 = (f32[1,1024]{1,0:T(1,128)S(1)}, f32[144,1024]{1,0:T(8,128)S(1)}) custom-call(bf16[1024,128]{1,0:T(8,128)(2,1)S(1)} %bitcast.22, bf16[4096,128]{1,0:T(8,128)(2,1)S(1)} %collective-permute-done.key_ref.other_key_ref, bf16[4096,128]{1,0:T(8,128)(2,1)S(1)} %collective-permute-done.1.value_ref.other_value_ref), custom_call_target="tpu_custom_call" | custom-call | flops 3221225472 | bytes 2097152 | tf_op jit(solution)/shard_map/prefix_first/pallas_call | solution.py:183
  29.4 0.0 copy-done.4
  29.4 0.0 copy-done.5
  29.4 0.0 copy-start.1
  29.4 0.0 copy-start.2
  29.4 0.0 copy-start.3
  29.4 4.6 %prefix_second.1 = bf16[16,80,128]{2,1,0:T(8,128)(2,1)} custom-call(bf16[1024,128]{1,0:T(8,128)(2,1)S(1)} %bitcast.23, bf16[4096,128]{1,0:T(8,128)(2,1)S(1)} %bitcast.31, bf16[4096,128]{1,0:T(8,128)(2,1)S(1)} %bitcast.33, bf16[4096,128]{1,0:T(8,128)(2,1)S(1)} %collective-permute-done.key_ref.other_key_ref, ...), custom_call_target="tpu_custom_call" | custom-call | flops 3221225472 | bytes 2097152 | tf_op jit(solution)/shard_map/prefix_second/pallas_call | solution.py:196
  34.1 60.4 %all-to-all-start.1 = ((bf16[16,80,128]{2,1,0:T(8,128)(2,1)}), bf16[16,80,128]{2,1,0:T(8,128)(2,1)S(1)}, u32[]{:S(2)}, u32[]{:S(2)}) async-start(bf16[16,80,128]{2,1,0:T(8,128)(2,1)} %prefix_second.1), calls=%async_computation.1 | async-start | bytes 655360 | tf_op jit(solution)/shard_map/all_to_all | solution.py:401
  94.5 0.0 copy-done.1
  94.5 0.0 copy-done.2
  94.5 0.0 copy-done.3
  94.6 6.7 %suffix_part.1 = (f32[4,16,128]{2,1,0:T(8,128)S(1)}, f32[4,16,128]{2,1,0:T(8,128)S(1)}, f32[4,16,128]{2,1,0:T(8,128)S(1)}) custom-call(s32[4]{0:T(128)S(1)} %copy-done.3, bf16[4,16,128]{2,1,0:T(8,128)(2,1)S(1)} %bitcast.24, bf16[4,2,128]{2,1,0:T(2,128)(2,1)S(1)} %bitcast.28, bf16[4,2,128]{2,1,0:T(2,128)(2,1)S(1)} %bitcast.29, ...), custom_call_target="tpu_custom_call" | custom-call | flops 134217728 | bytes 8388608 | tf_op jit(solution)/shard_map/suffix_part/pallas_call | solution.py:319
  101.3 5.7 %all-to-all-done.1.part_ref = bf16[16,80,128]{2,1,0:T(8,128)(2,1)S(1)} async-done(((bf16[16,80,128]{2,1,0:T(8,128)(2,1)}), bf16[16,80,128]{2,1,0:T(8,128)(2,1)S(1)}, u32[]{:S(2)}, u32[]{:S(2)}) %all-to-all-start.1) | async-done | bytes 327712 | tf_op jit(solution)/shard_map/all_to_all | solution.py:401
  106.9 0.7 combine_parts.1
  107.6 15.0 %all_to_all.28 = bf16[16,8,1024]{2,1,0:T(8,128)(2,1)S(1)} all-to-all(bf16[16,8,1024]{2,1,0:T(8,128)(2,1)S(1)} %tile.5), channel_id=1, replica_groups={{0,16,32,48,64,80,96,112,128,144,160,176,192,208,224,240},{8,24,40,56,7..., dimensions={0} | all-to-all | bytes 524288 | tf_op jit(solution)/shard_map/all_to_all | solution.py:406
  122.6 3.5 %collective-permute-start.2 = (bf16[128,1024]{1,0:T(8,128)(2,1)S(1)}, bf16[128,1024]{1,0:T(8,128)(2,1)S(1)}, u32[]{:S(2)}, u32[]{:S(2)}) collective-permute-start(bf16[128,1024]{1,0:T(8,128)(2,1)S(1)} %bitcast.37), channel_id=1, source_target_pairs={{0,8},{8,0},{16,24},{24,16},{32,40},{40,32},{48,56},{56,48},{64,72... | collective-permute-start | bytes 786440 | tf_op jit(solution)/shard_map/ppermute | solution.py:409
  126.1 1.2 collective-permute-done.2
  127.3 0.1 pad_maximum_fusion
  127.4 0.0 copy-done
  127.4 0.3 convolution_convert_fusion
  127.7 9.5 %all_to_all.29 = bf16[8,32,256]{2,1,0:T(8,128)(2,1)S(1)} all-to-all(bf16[8,32,256]{2,1,0:T(8,128)(2,1)S(1)} %bitcast.38), channel_id=1, replica_groups=mesh['seq'=32,'head'=8] {'head'}, dimensions={0} | all-to-all | bytes 262144 | tf_op jit(solution)/shard_map/all_to_all | solution.py:420
  137.3 0.6 reshape.45
  (4 shorter events, 0.1 us)
Async XLA Ops:
  0.0 127.4 %copy-start = (bf16[1024,256]{1,0:T(8,128)(2,1)S(1)}, bf16[1024,256]{1,0:T(8,128)(2,1)}, u32[]{:S(2)}) copy-start(bf16[1024,256]{1,0:T(8,128)(2,1)} %param.17) | copy-start | bytes 1572868
  0.0 25.4 %collective-permute-start = (bf16[4096,128]{1,0:T(8,128)(2,1)}, bf16[4096,128]{1,0:T(8,128)(2,1)S(1)}, u32[]{:S(2)}, u32[]{:S(2)}) collective-permute-start(bf16[4096,128]{1,0:T(8,128)(2,1)} %bitcast.30), channel_id=1, source_target_pairs={{0,8},{8,0},{16,24},{24,16},{32,40},{40,32},{48,56},{56,48},{64,72... | collective-permute-start | bytes 3145736 | tf_op jit(solution)/shard_map/ppermute | solution.py:393
  3.2 22.1 %collective-permute-start.1 = (bf16[4096,128]{1,0:T(8,128)(2,1)}, bf16[4096,128]{1,0:T(8,128)(2,1)S(1)}, u32[]{:S(2)}, u32[]{:S(2)}) collective-permute-start(bf16[4096,128]{1,0:T(8,128)(2,1)} %bitcast.32), channel_id=1, source_target_pairs={{0,8},{8,0},{16,24},{24,16},{32,40},{40,32},{48,56},{56,48},{64,72... | collective-permute-start | bytes 3145736 | tf_op jit(solution)/shard_map/ppermute | solution.py:394
  25.4 4.0 %copy-start.4 = (bf16[4096,1,128]{2,0,1:T(8,128)(2,1)S(1)}, bf16[4096,1,128]{2,0,1:T(8,128)(2,1)}, u32[]{:S(2)}) copy-start(bf16[4096,1,128]{2,0,1:T(8,128)(2,1)} %param.10) | copy-start | bytes 3145732
  25.4 4.0 %copy-start.5 = (bf16[4096,1,128]{2,0,1:T(8,128)(2,1)S(1)}, bf16[4096,1,128]{2,0,1:T(8,128)(2,1)}, u32[]{:S(2)}) copy-start(bf16[4096,1,128]{2,0,1:T(8,128)(2,1)} %param.11) | copy-start | bytes 3145732
  29.4 65.1 %copy-start.1 = (bf16[4,2,1,128]{3,1,2,0:T(2,128)(2,1)S(1)}, bf16[4,2,1,128]{3,1,2,0:T(2,128)(2,1)}, u32[]{:S(2)}) copy-start(bf16[4,2,1,128]{3,1,2,0:T(2,128)(2,1)} %param.14) | copy-start | bytes 6148
  29.4 65.1 %copy-start.2 = (bf16[4,2,1,128]{3,1,2,0:T(2,128)(2,1)S(1)}, bf16[4,2,1,128]{3,1,2,0:T(2,128)(2,1)}, u32[]{:S(2)}) copy-start(bf16[4,2,1,128]{3,1,2,0:T(2,128)(2,1)} %param.15) | copy-start | bytes 6148
  29.4 65.1 %copy-start.3 = (s32[4]{0:T(128)S(1)}, s32[4]{0:T(128)}, u32[]{:S(2)}) copy-start(s32[4]{0:T(128)} %length_ref.1) | copy-start | bytes 52
  34.1 72.8 %all-to-all-start.1 = ((bf16[16,80,128]{2,1,0:T(8,128)(2,1)}), bf16[16,80,128]{2,1,0:T(8,128)(2,1)S(1)}, u32[]{:S(2)}, u32[]{:S(2)}) async-start(bf16[16,80,128]{2,1,0:T(8,128)(2,1)} %prefix_second.1), calls=%async_computation.1 | async-start | bytes 655360 | tf_op jit(solution)/shard_map/all_to_all | solution.py:401
  122.6 4.7 %collective-permute-start.2 = (bf16[128,1024]{1,0:T(8,128)(2,1)S(1)}, bf16[128,1024]{1,0:T(8,128)(2,1)S(1)}, u32[]{:S(2)}, u32[]{:S(2)}) collective-permute-start(bf16[128,1024]{1,0:T(8,128)(2,1)S(1)} %bitcast.37), channel_id=1, source_target_pairs={{0,8},{8,0},{16,24},{24,16},{32,40},{40,32},{48,56},{56,48},{64,72... | collective-permute-start | bytes 786440 | tf_op jit(solution)/shard_map/ppermute | solution.py:409

commit v3 on v2

--- a/solution.py
+++ b/solution.py
@@ -96,10 +96,11 @@
 
 def write_columns(out_ref, first, group, top, total, acc):
     head_dim = acc.shape[0]
+    inverse = 1.0 / total
     lane = lax.broadcasted_iota(jnp.int32, (STAT_ROWS, head_dim), 1)
     for index in range(acc.shape[1] // head_dim):
         lanes = slice(index * head_dim, (index + 1) * head_dim)
-        mean = (acc[:, lanes] / total[:, lanes]).T.astype(jnp.bfloat16)
+        mean = (acc[:, lanes] * inverse[:, lanes]).T.astype(jnp.bfloat16)
         tops = jnp.broadcast_to(top[:, lanes], (STAT_ROWS, head_dim))
         totals = jnp.broadcast_to(total[:, lanes], (STAT_ROWS, head_dim))
         stats = (
@@ -174,7 +175,7 @@
     held = pl.BlockSpec(memory_space=pltpu.VMEM)
     limit = pltpu.CompilerParams(vmem_limit_bytes=32 * 2**20)
     key_block = min(256, positions)
-    chunk = min(256, count)
+    chunk = min(512, count)
     cost = pl.CostEstimate(
         flops=6 * count * positions * head_dim,
         bytes_accessed=4 * positions * head_dim,
@@ -350,7 +351,7 @@
     acc = mean_ref[...] * own
     for sender in range(senders):
         acc = acc + part_ref[sender, :rows, :].astype(jnp.float32) * weights[:, sender : sender + 1]
-    acc_ref[...] = acc / total
+    acc_ref[...] = acc * (1.0 / total)
     for head in range(heads):
         out_ref[:, head * head_dim : (head + 1) * head_dim] = acc_ref[
             pl.ds(head, lines, stride=heads), :
@@ -369,6 +370,29 @@
         compiler_params=pltpu.CompilerParams(vmem_limit_bytes=16 * 2**20),
         name="combine_parts",
     )(parts, mean, top, total)
+
+
+def head_sum_kernel(part_ref, out_ref):
+    total = part_ref[0].astype(jnp.float32)
+    for head in range(1, part_ref.shape[0]):
+        total = total + part_ref[head].astype(jnp.float32)
+    steps = out_ref.shape[1]
+    for request in range(out_ref.shape[0]):
+        rows = total[request * steps : (request + 1) * steps]
+        out_ref[request] = rows.astype(jnp.bfloat16)
+
+
+def head_sum(parts, steps):
+    _, rows, columns = parts.shape
+    held = pl.BlockSpec(memory_space=pltpu.VMEM)
+    return pl.pallas_call(
+        head_sum_kernel,
+        in_specs=[held],
+        out_specs=held,
+        out_shape=jax.ShapeDtypeStruct((rows // steps, steps, columns), jnp.bfloat16),
+        compiler_params=pltpu.CompilerParams(vmem_limit_bytes=16 * 2**20),
+        name="head_sum",
+    )(parts)
 
 
 def shards(
@@ -418,8 +442,7 @@
     heads = lax.axis_size("head")
     partial = partial.astype(jnp.bfloat16).reshape(heads, everyone * steps // heads, columns)
     partial = lax.all_to_all(partial, "head", 0, 0, tiled=True)
-    summed = jnp.sum(partial.astype(jnp.float32), axis=0).astype(jnp.bfloat16)
-    return summed.reshape(everyone // heads, steps, columns)
+    return head_sum(partial, steps)
 
 
 def solution(mesh):

time: 138 us -> 117 us (0.85)
  starting transfers between devices: 67.2 us -> 46.4 us
    all_to_all x1, starting transfers between devices: 60.4 us -> 39.7 us  [shards(): lax.all_to_all(parts, 'seq', 0, 0, axis_index_groups=same_core, tiled=True)]
  transfers between devices with their start and end apart: 4 -> 4, of which waited for: 2 -> 2; matrix products, arithmetic and copies ran while one was open for 1% -> 1% of each run, Pallas kernels for 5% -> 6%
where the time goes in v3:
time: 117 us
  starting transfers between devices  46.4 us (40%)
  blocking collectives  45.9 us (39%)
  Pallas kernels  16.6 us (14%)
  waiting for transfers between devices  6.83 us (6%)
    all_to_all x1, starting transfers between devices, shards(): lax.all_to_all(parts, 'seq', 0, 0, axis_index_groups=same_core, tiled=True)  39.7 us
    all_to_all x1, blocking collectives, shards(): lax.all_to_all(jnp.tile(own_rows, (sharers, 1)), 'seq', 0, 0, axis_index_...  21.3 us
    all_to_all x1, blocking collectives, shards(): lax.all_to_all(jnp.tile(attended, (sharers, 1)), 'seq', 0, 0, axis_index_...  15 us
    all_to_all x1, blocking collectives, shards(): partial = lax.all_to_all(partial, 'head', 0, 0, tiled=True)  9.51 us
    pallas_call x1, Pallas kernels, suffix_part(): pl.pallas_call(functools.partial(suffix_kernel, key_block=key_block, grou...  6.7 us
    all_to_all x1, waiting for transfers between devices, shards(): lax.all_to_all(parts, 'seq', 0, 0, axis_index_groups=same_core, tiled=True)  5.66 us
    pallas_call x1, Pallas kernels, prefix_parts(): pl.pallas_call(functools.partial(second_kernel, chunk=chunk, key_block=ke...  4.63 us
    pallas_call x1, Pallas kernels, prefix_parts(): pl.pallas_call(functools.partial(first_kernel, key_block=key_block, scale...  4.01 us
  transfers between devices with their start and end apart: 4, of which 2 were waited for; matrix products, arithmetic and copies ran while one was open for 1% of the time, Pallas kernels for 6%

profile of v3, /device:TPU:1, one launch (start us, length us, event | category | flops | bytes accessed | tf_op | source)
XLA Modules:
  0.0 117.1 jit_solution(1962997134868941383)
XLA Ops:
  0.0 0.0 copy-start
  0.0 3.2 %collective-permute-start = (bf16[4096,128]{1,0:T(8,128)(2,1)}, bf16[4096,128]{1,0:T(8,128)(2,1)S(1)}, u32[]{:S(2)}, u32[]{:S(2)}) collective-permute-start(bf16[4096,128]{1,0:T(8,128)(2,1)} %bitcast.30), channel_id=1, source_target_pairs={{0,8},{8,0},{16,24},{24,16},{32,40},{40,32},{48,56},{56,48},{64,72... | collective-permute-start | bytes 3145736 | tf_op jit(solution)/shard_map/ppermute | solution.py:417
  3.2 0.0 collective-permute-start.1
  3.2 0.7 reshape.35
  4.0 21.3 %all_to_all.27 = bf16[16,64,128]{2,1,0:T(8,128)(2,1)S(1)} all-to-all(bf16[16,64,128]{2,1,0:T(8,128)(2,1)S(1)} %tile.4), channel_id=1, replica_groups={{0,16,32,48,64,80,96,112,128,144,160,176,192,208,224,240},{8,24,40,56,7..., dimensions={0} | all-to-all | bytes 524288 | tf_op jit(solution)/shard_map/all_to_all | solution.py:414
  25.4 0.0 collective-permute-done.key_ref.other_key_ref
  25.4 0.0 collective-permute-done.1.value_ref.other_value_ref
  25.4 0.0 copy-start.4
  25.4 0.0 copy-start.5
  25.4 4.0 %prefix_first.1 = (f32[1,1024]{1,0:T(1,128)S(1)}, f32[144,1024]{1,0:T(8,128)S(1)}) custom-call(bf16[1024,128]{1,0:T(8,128)(2,1)S(1)} %bitcast.22, bf16[4096,128]{1,0:T(8,128)(2,1)S(1)} %collective-permute-done.key_ref.other_key_ref, bf16[4096,128]{1,0:T(8,128)(2,1)S(1)} %collective-permute-done.1.value_ref.other_value_ref), custom_call_target="tpu_custom_call" | custom-call | flops 3221225472 | bytes 2097152 | tf_op jit(solution)/shard_map/prefix_first/pallas_call | solution.py:184
  29.4 0.0 copy-done.4
  29.4 0.0 copy-done.5
  29.4 0.0 copy-start.1
  29.4 0.0 copy-start.2
  29.4 0.0 copy-start.3
  29.4 4.6 %prefix_second.1 = bf16[16,80,128]{2,1,0:T(8,128)(2,1)} custom-call(bf16[1024,128]{1,0:T(8,128)(2,1)S(1)} %bitcast.23, bf16[4096,128]{1,0:T(8,128)(2,1)S(1)} %bitcast.31, bf16[4096,128]{1,0:T(8,128)(2,1)S(1)} %bitcast.33, bf16[4096,128]{1,0:T(8,128)(2,1)S(1)} %collective-permute-done.key_ref.other_key_ref, ...), custom_call_target="tpu_custom_call" | custom-call | flops 3221225472 | bytes 2097152 | tf_op jit(solution)/shard_map/prefix_second/pallas_call | solution.py:197
  34.1 39.7 %all-to-all-start.1 = ((bf16[16,80,128]{2,1,0:T(8,128)(2,1)}), bf16[16,80,128]{2,1,0:T(8,128)(2,1)S(1)}, u32[]{:S(2)}, u32[]{:S(2)}) async-start(bf16[16,80,128]{2,1,0:T(8,128)(2,1)} %prefix_second.1), calls=%async_computation.1 | async-start | bytes 655360 | tf_op jit(solution)/shard_map/all_to_all | solution.py:425
  73.8 0.0 copy-done.1
  73.8 0.0 copy-done.2
  73.8 0.0 copy-done.3
  73.8 6.7 %suffix_part.1 = (f32[4,16,128]{2,1,0:T(8,128)S(1)}, f32[4,16,128]{2,1,0:T(8,128)S(1)}, f32[4,16,128]{2,1,0:T(8,128)S(1)}) custom-call(s32[4]{0:T(128)S(1)} %copy-done.3, bf16[4,16,128]{2,1,0:T(8,128)(2,1)S(1)} %bitcast.24, bf16[4,2,128]{2,1,0:T(2,128)(2,1)S(1)} %bitcast.28, bf16[4,2,128]{2,1,0:T(2,128)(2,1)S(1)} %bitcast.29, ...), custom_call_target="tpu_custom_call" | custom-call | flops 134217728 | bytes 8388608 | tf_op jit(solution)/shard_map/suffix_part/pallas_call | solution.py:320
  80.5 5.7 %all-to-all-done.1.part_ref = bf16[16,80,128]{2,1,0:T(8,128)(2,1)S(1)} async-done(((bf16[16,80,128]{2,1,0:T(8,128)(2,1)}), bf16[16,80,128]{2,1,0:T(8,128)(2,1)S(1)}, u32[]{:S(2)}, u32[]{:S(2)}) %all-to-all-start.1) | async-done | bytes 327712 | tf_op jit(solution)/shard_map/all_to_all | solution.py:425
  86.2 0.6 combine_parts.1
  86.9 15.0 %all_to_all.28 = bf16[16,8,1024]{2,1,0:T(8,128)(2,1)S(1)} all-to-all(bf16[16,8,1024]{2,1,0:T(8,128)(2,1)S(1)} %tile.5), channel_id=1, replica_groups={{0,16,32,48,64,80,96,112,128,144,160,176,192,208,224,240},{8,24,40,56,7..., dimensions={0} | all-to-all | bytes 524288 | tf_op jit(solution)/shard_map/all_to_all | solution.py:430
  101.9 3.5 %collective-permute-start.2 = (bf16[128,1024]{1,0:T(8,128)(2,1)S(1)}, bf16[128,1024]{1,0:T(8,128)(2,1)S(1)}, u32[]{:S(2)}, u32[]{:S(2)}) collective-permute-start(bf16[128,1024]{1,0:T(8,128)(2,1)S(1)} %bitcast.37), channel_id=1, source_target_pairs={{0,8},{8,0},{16,24},{24,16},{32,40},{40,32},{48,56},{56,48},{64,72... | collective-permute-start | bytes 786440 | tf_op jit(solution)/shard_map/ppermute | solution.py:433
  105.4 1.2 collective-permute-done.2
  106.6 0.1 pad_maximum_fusion
  106.6 0.0 copy-done
  106.7 0.3 convolution_convert_fusion
  107.0 9.5 %all_to_all.29.part_ref = bf16[8,32,256]{2,1,0:T(8,128)(2,1)S(1)} all-to-all(bf16[8,32,256]{2,1,0:T(8,128)(2,1)S(1)} %bitcast.38), channel_id=1, replica_groups=mesh['seq'=32,'head'=8] {'head'}, dimensions={0} | all-to-all | bytes 262144 | tf_op jit(solution)/shard_map/all_to_all | solution.py:444
  116.5 0.6 head_sum.1
  (3 shorter events, 0.1 us)
Async XLA Ops:
  0.0 106.6 %copy-start = (bf16[1024,256]{1,0:T(8,128)(2,1)S(1)}, bf16[1024,256]{1,0:T(8,128)(2,1)}, u32[]{:S(2)}) copy-start(bf16[1024,256]{1,0:T(8,128)(2,1)} %param.17) | copy-start | bytes 1572868
  0.0 25.4 %collective-permute-start = (bf16[4096,128]{1,0:T(8,128)(2,1)}, bf16[4096,128]{1,0:T(8,128)(2,1)S(1)}, u32[]{:S(2)}, u32[]{:S(2)}) collective-permute-start(bf16[4096,128]{1,0:T(8,128)(2,1)} %bitcast.30), channel_id=1, source_target_pairs={{0,8},{8,0},{16,24},{24,16},{32,40},{40,32},{48,56},{56,48},{64,72... | collective-permute-start | bytes 3145736 | tf_op jit(solution)/shard_map/ppermute | solution.py:417
  3.2 22.1 %collective-permute-start.1 = (bf16[4096,128]{1,0:T(8,128)(2,1)}, bf16[4096,128]{1,0:T(8,128)(2,1)S(1)}, u32[]{:S(2)}, u32[]{:S(2)}) collective-permute-start(bf16[4096,128]{1,0:T(8,128)(2,1)} %bitcast.32), channel_id=1, source_target_pairs={{0,8},{8,0},{16,24},{24,16},{32,40},{40,32},{48,56},{56,48},{64,72... | collective-permute-start | bytes 3145736 | tf_op jit(solution)/shard_map/ppermute | solution.py:418
  25.4 4.0 %copy-start.4 = (bf16[4096,1,128]{2,0,1:T(8,128)(2,1)S(1)}, bf16[4096,1,128]{2,0,1:T(8,128)(2,1)}, u32[]{:S(2)}) copy-start(bf16[4096,1,128]{2,0,1:T(8,128)(2,1)} %param.10) | copy-start | bytes 3145732
  25.4 4.0 %copy-start.5 = (bf16[4096,1,128]{2,0,1:T(8,128)(2,1)S(1)}, bf16[4096,1,128]{2,0,1:T(8,128)(2,1)}, u32[]{:S(2)}) copy-start(bf16[4096,1,128]{2,0,1:T(8,128)(2,1)} %param.11) | copy-start | bytes 3145732
  29.4 44.4 %copy-start.1 = (bf16[4,2,1,128]{3,1,2,0:T(2,128)(2,1)S(1)}, bf16[4,2,1,128]{3,1,2,0:T(2,128)(2,1)}, u32[]{:S(2)}) copy-start(bf16[4,2,1,128]{3,1,2,0:T(2,128)(2,1)} %param.14) | copy-start | bytes 6148
  29.4 44.4 %copy-start.2 = (bf16[4,2,1,128]{3,1,2,0:T(2,128)(2,1)S(1)}, bf16[4,2,1,128]{3,1,2,0:T(2,128)(2,1)}, u32[]{:S(2)}) copy-start(bf16[4,2,1,128]{3,1,2,0:T(2,128)(2,1)} %param.15) | copy-start | bytes 6148
  29.4 44.4 %copy-start.3 = (s32[4]{0:T(128)S(1)}, s32[4]{0:T(128)}, u32[]{:S(2)}) copy-start(s32[4]{0:T(128)} %length_ref.1) | copy-start | bytes 52
  34.1 52.1 %all-to-all-start.1 = ((bf16[16,80,128]{2,1,0:T(8,128)(2,1)}), bf16[16,80,128]{2,1,0:T(8,128)(2,1)S(1)}, u32[]{:S(2)}, u32[]{:S(2)}) async-start(bf16[16,80,128]{2,1,0:T(8,128)(2,1)} %prefix_second.1), calls=%async_computation.1 | async-start | bytes 655360 | tf_op jit(solution)/shard_map/all_to_all | solution.py:425
  101.9 4.7 %collective-permute-start.2 = (bf16[128,1024]{1,0:T(8,128)(2,1)S(1)}, bf16[128,1024]{1,0:T(8,128)(2,1)S(1)}, u32[]{:S(2)}, u32[]{:S(2)}) collective-permute-start(bf16[128,1024]{1,0:T(8,128)(2,1)S(1)} %bitcast.37), channel_id=1, source_target_pairs={{0,8},{8,0},{16,24},{24,16},{32,40},{40,32},{48,56},{56,48},{64,72... | collective-permute-start | bytes 786440 | tf_op jit(solution)/shard_map/ppermute | solution.py:433

commit v4 on v3

--- a/solution.py
+++ b/solution.py
@@ -337,7 +337,7 @@
 def combine_kernel(part_ref, mean_ref, top_ref, total_ref, out_ref, acc_ref):
     senders, height, head_dim = part_ref.shape
     rows = height - STAT_ROWS
-    lines = out_ref.shape[0]
+    lines = out_ref.shape[1]
     heads = rows // lines
     stat = jnp.sum(part_ref[:, rows : rows + STAT_ROWS, :].astype(jnp.float32), axis=1)
     stat = stat.T
@@ -353,19 +353,19 @@
         acc = acc + part_ref[sender, :rows, :].astype(jnp.float32) * weights[:, sender : sender + 1]
     acc_ref[...] = acc * (1.0 / total)
     for head in range(heads):
-        out_ref[:, head * head_dim : (head + 1) * head_dim] = acc_ref[
-            pl.ds(head, lines, stride=heads), :
-        ].astype(jnp.bfloat16)
-
-
-def combine(parts, mean, top, total, lines):
+        part = acc_ref[pl.ds(head, lines, stride=heads), :].astype(jnp.bfloat16)
+        for copy in range(out_ref.shape[0]):
+            out_ref[copy, :, head * head_dim : (head + 1) * head_dim] = part
+
+
+def combine(parts, mean, top, total, lines, copies):
     rows, head_dim = mean.shape
     held = pl.BlockSpec(memory_space=pltpu.VMEM)
     return pl.pallas_call(
         combine_kernel,
         in_specs=[held] * 4,
         out_specs=held,
-        out_shape=jax.ShapeDtypeStruct((lines, rows // lines * head_dim), jnp.bfloat16),
+        out_shape=jax.ShapeDtypeStruct((copies, lines, rows // lines * head_dim), jnp.bfloat16),
         scratch_shapes=[pltpu.VMEM((rows, head_dim), jnp.float32)],
         compiler_params=pltpu.CompilerParams(vmem_limit_bytes=16 * 2**20),
         name="combine_parts",
@@ -425,11 +425,11 @@
     parts = lax.all_to_all(parts, "seq", 0, 0, axis_index_groups=same_core, tiled=True)
     attended = combine(
         parts, mean.reshape(group, head_dim), top.reshape(group, head_dim),
-        total.reshape(group, head_dim), owned * steps,
+        total.reshape(group, head_dim), owned * steps, sharers,
     )
     attended = lax.all_to_all(
-        jnp.tile(attended, (sharers, 1)), "seq", 0, 0, axis_index_groups=same_core, tiled=True
-    )
+        attended, "seq", 0, 0, axis_index_groups=same_core, tiled=True
+    ).reshape(sharers * owned * steps, row_width)
     other_attended = lax.ppermute(attended, "seq", swap_cores)
     core = lax.axis_index("seq") % 2
     even = jnp.where(core == 0, attended, other_attended)

time: 117 us -> 117 us (level)
  no operation moved by 1% of the time
where the time goes in v4:
time: 117 us
  starting transfers between devices  46.4 us (40%)
  blocking collectives  45.9 us (39%)
  Pallas kernels  16.7 us (14%)
  waiting for transfers between devices  6.83 us (6%)
    all_to_all x1, starting transfers between devices, shards(): lax.all_to_all(parts, 'seq', 0, 0, axis_index_groups=same_core, tiled=True)  39.7 us
    all_to_all x1, blocking collectives, shards(): lax.all_to_all(jnp.tile(own_rows, (sharers, 1)), 'seq', 0, 0, axis_index_...  21.3 us
    all_to_all x1, blocking collectives, shards(): lax.all_to_all(attended, 'seq', 0, 0, axis_index_groups=same_core, tiled=...  15 us
    all_to_all x1, blocking collectives, shards(): partial = lax.all_to_all(partial, 'head', 0, 0, tiled=True)  9.51 us
    pallas_call x1, Pallas kernels, suffix_part(): pl.pallas_call(functools.partial(suffix_kernel, key_block=key_block, grou...  6.7 us
    all_to_all x1, waiting for transfers between devices, shards(): lax.all_to_all(parts, 'seq', 0, 0, axis_index_groups=same_core, tiled=True)  5.66 us
    pallas_call x1, Pallas kernels, prefix_parts(): pl.pallas_call(functools.partial(second_kernel, chunk=chunk, key_block=ke...  4.63 us
    pallas_call x1, Pallas kernels, prefix_parts(): pl.pallas_call(functools.partial(first_kernel, key_block=key_block, scale...  4.01 us
  transfers between devices with their start and end apart: 4, of which 2 were waited for; matrix products, arithmetic and copies ran while one was open for 1% of the time, Pallas kernels for 6%

profile of v4, /device:TPU:1, one launch (start us, length us, event | category | flops | bytes accessed | tf_op | source)
XLA Modules:
  0.0 117.1 jit_solution(14544620605879446569)
XLA Ops:
  0.0 0.0 copy-start
  0.0 3.2 %collective-permute-start = (bf16[4096,128]{1,0:T(8,128)(2,1)}, bf16[4096,128]{1,0:T(8,128)(2,1)S(1)}, u32[]{:S(2)}, u32[]{:S(2)}) collective-permute-start(bf16[4096,128]{1,0:T(8,128)(2,1)} %bitcast.30), channel_id=1, source_target_pairs={{0,8},{8,0},{16,24},{24,16},{32,40},{40,32},{48,56},{56,48},{64,72... | collective-permute-start | bytes 3145736 | tf_op jit(solution)/shard_map/ppermute | solution.py:417
  3.2 0.0 collective-permute-start.1
  3.2 0.7 reshape.31
  4.0 21.3 %all_to_all.23 = bf16[16,64,128]{2,1,0:T(8,128)(2,1)S(1)} all-to-all(bf16[16,64,128]{2,1,0:T(8,128)(2,1)S(1)} %tile.2), channel_id=1, replica_groups={{0,16,32,48,64,80,96,112,128,144,160,176,192,208,224,240},{8,24,40,56,7..., dimensions={0} | all-to-all | bytes 524288 | tf_op jit(solution)/shard_map/all_to_all | solution.py:414
  25.4 0.0 collective-permute-done.key_ref.other_key_ref
  25.4 0.0 collective-permute-done.1.value_ref.other_value_ref
  25.4 0.0 copy-start.4
  25.4 0.0 copy-start.5
  25.4 4.0 %prefix_first.1 = (f32[1,1024]{1,0:T(1,128)S(1)}, f32[144,1024]{1,0:T(8,128)S(1)}) custom-call(bf16[1024,128]{1,0:T(8,128)(2,1)S(1)} %bitcast.22, bf16[4096,128]{1,0:T(8,128)(2,1)S(1)} %collective-permute-done.key_ref.other_key_ref, bf16[4096,128]{1,0:T(8,128)(2,1)S(1)} %collective-permute-done.1.value_ref.other_value_ref), custom_call_target="tpu_custom_call" | custom-call | flops 3221225472 | bytes 2097152 | tf_op jit(solution)/shard_map/prefix_first/pallas_call | solution.py:184
  29.4 0.0 copy-done.4
  29.4 0.0 copy-done.5
  29.4 0.0 copy-start.1
  29.4 0.0 copy-start.2
  29.4 0.0 copy-start.3
  29.4 4.6 %prefix_second.1 = bf16[16,80,128]{2,1,0:T(8,128)(2,1)} custom-call(bf16[1024,128]{1,0:T(8,128)(2,1)S(1)} %bitcast.23, bf16[4096,128]{1,0:T(8,128)(2,1)S(1)} %bitcast.31, bf16[4096,128]{1,0:T(8,128)(2,1)S(1)} %bitcast.33, bf16[4096,128]{1,0:T(8,128)(2,1)S(1)} %collective-permute-done.key_ref.other_key_ref, ...), custom_call_target="tpu_custom_call" | custom-call | flops 3221225472 | bytes 2097152 | tf_op jit(solution)/shard_map/prefix_second/pallas_call | solution.py:197
  34.1 39.7 %all-to-all-start.1 = ((bf16[16,80,128]{2,1,0:T(8,128)(2,1)}), bf16[16,80,128]{2,1,0:T(8,128)(2,1)S(1)}, u32[]{:S(2)}, u32[]{:S(2)}) async-start(bf16[16,80,128]{2,1,0:T(8,128)(2,1)} %prefix_second.1), calls=%async_computation.1 | async-start | bytes 655360 | tf_op jit(solution)/shard_map/all_to_all | solution.py:425
  73.8 0.0 copy-done.1
  73.8 0.0 copy-done.2
  73.8 0.0 copy-done.3
  73.8 6.7 %suffix_part.1 = (f32[4,16,128]{2,1,0:T(8,128)S(1)}, f32[4,16,128]{2,1,0:T(8,128)S(1)}, f32[4,16,128]{2,1,0:T(8,128)S(1)}) custom-call(s32[4]{0:T(128)S(1)} %copy-done.3, bf16[4,16,128]{2,1,0:T(8,128)(2,1)S(1)} %bitcast.24, bf16[4,2,128]{2,1,0:T(2,128)(2,1)S(1)} %bitcast.28, bf16[4,2,128]{2,1,0:T(2,128)(2,1)S(1)} %bitcast.29, ...), custom_call_target="tpu_custom_call" | custom-call | flops 134217728 | bytes 8388608 | tf_op jit(solution)/shard_map/suffix_part/pallas_call | solution.py:320
  80.5 5.7 %all-to-all-done.1.part_ref = bf16[16,80,128]{2,1,0:T(8,128)(2,1)S(1)} async-done(((bf16[16,80,128]{2,1,0:T(8,128)(2,1)}), bf16[16,80,128]{2,1,0:T(8,128)(2,1)S(1)}, u32[]{:S(2)}, u32[]{:S(2)}) %all-to-all-start.1) | async-done | bytes 327712 | tf_op jit(solution)/shard_map/all_to_all | solution.py:425
  86.2 0.7 combine_parts.1
  86.9 15.0 %all_to_all.24 = bf16[16,8,1024]{2,1,0:T(8,128)(2,1)S(1)} all-to-all(bf16[16,8,1024]{2,1,0:T(8,128)(2,1)S(1)} %combine_parts.1), channel_id=1, replica_groups={{0,16,32,48,64,80,96,112,128,144,160,176,192,208,224,240},{8,24,40,56,7..., dimensions={0} | all-to-all | bytes 524288 | tf_op jit(solution)/shard_map/all_to_all | solution.py:430
  101.9 3.5 %collective-permute-start.2 = (bf16[128,1024]{1,0:T(8,128)(2,1)S(1)}, bf16[128,1024]{1,0:T(8,128)(2,1)S(1)}, u32[]{:S(2)}, u32[]{:S(2)}) collective-permute-start(bf16[128,1024]{1,0:T(8,128)(2,1)S(1)} %bitcast.37), channel_id=1, source_target_pairs={{0,8},{8,0},{16,24},{24,16},{32,40},{40,32},{48,56},{56,48},{64,72... | collective-permute-start | bytes 786440 | tf_op jit(solution)/shard_map/ppermute | solution.py:433
  105.4 1.2 collective-permute-done.2
  106.6 0.1 pad_maximum_fusion
  106.7 0.0 copy-done
  106.7 0.3 convolution_convert_fusion
  107.0 9.5 %all_to_all.25.part_ref = bf16[8,32,256]{2,1,0:T(8,128)(2,1)S(1)} all-to-all(bf16[8,32,256]{2,1,0:T(8,128)(2,1)S(1)} %bitcast.38), channel_id=1, replica_groups=mesh['seq'=32,'head'=8] {'head'}, dimensions={0} | all-to-all | bytes 262144 | tf_op jit(solution)/shard_map/all_to_all | solution.py:444
  116.5 0.6 head_sum.1
  (2 shorter events, 0.1 us)
Async XLA Ops:
  0.0 106.7 %copy-start = (bf16[1024,256]{1,0:T(8,128)(2,1)S(1)}, bf16[1024,256]{1,0:T(8,128)(2,1)}, u32[]{:S(2)}) copy-start(bf16[1024,256]{1,0:T(8,128)(2,1)} %param.17) | copy-start | bytes 1572868
  0.0 25.4 %collective-permute-start = (bf16[4096,128]{1,0:T(8,128)(2,1)}, bf16[4096,128]{1,0:T(8,128)(2,1)S(1)}, u32[]{:S(2)}, u32[]{:S(2)}) collective-permute-start(bf16[4096,128]{1,0:T(8,128)(2,1)} %bitcast.30), channel_id=1, source_target_pairs={{0,8},{8,0},{16,24},{24,16},{32,40},{40,32},{48,56},{56,48},{64,72... | collective-permute-start | bytes 3145736 | tf_op jit(solution)/shard_map/ppermute | solution.py:417
  3.2 22.1 %collective-permute-start.1 = (bf16[4096,128]{1,0:T(8,128)(2,1)}, bf16[4096,128]{1,0:T(8,128)(2,1)S(1)}, u32[]{:S(2)}, u32[]{:S(2)}) collective-permute-start(bf16[4096,128]{1,0:T(8,128)(2,1)} %bitcast.32), channel_id=1, source_target_pairs={{0,8},{8,0},{16,24},{24,16},{32,40},{40,32},{48,56},{56,48},{64,72... | collective-permute-start | bytes 3145736 | tf_op jit(solution)/shard_map/ppermute | solution.py:418
  25.4 4.0 %copy-start.4 = (bf16[4096,1,128]{2,0,1:T(8,128)(2,1)S(1)}, bf16[4096,1,128]{2,0,1:T(8,128)(2,1)}, u32[]{:S(2)}) copy-start(bf16[4096,1,128]{2,0,1:T(8,128)(2,1)} %param.10) | copy-start | bytes 3145732
  25.4 4.0 %copy-start.5 = (bf16[4096,1,128]{2,0,1:T(8,128)(2,1)S(1)}, bf16[4096,1,128]{2,0,1:T(8,128)(2,1)}, u32[]{:S(2)}) copy-start(bf16[4096,1,128]{2,0,1:T(8,128)(2,1)} %param.11) | copy-start | bytes 3145732
  29.4 44.4 %copy-start.1 = (bf16[4,2,1,128]{3,1,2,0:T(2,128)(2,1)S(1)}, bf16[4,2,1,128]{3,1,2,0:T(2,128)(2,1)}, u32[]{:S(2)}) copy-start(bf16[4,2,1,128]{3,1,2,0:T(2,128)(2,1)} %param.14) | copy-start | bytes 6148
  29.4 44.4 %copy-start.2 = (bf16[4,2,1,128]{3,1,2,0:T(2,128)(2,1)S(1)}, bf16[4,2,1,128]{3,1,2,0:T(2,128)(2,1)}, u32[]{:S(2)}) copy-start(bf16[4,2,1,128]{3,1,2,0:T(2,128)(2,1)} %param.15) | copy-start | bytes 6148
  29.4 44.4 %copy-start.3 = (s32[4]{0:T(128)S(1)}, s32[4]{0:T(128)}, u32[]{:S(2)}) copy-start(s32[4]{0:T(128)} %length_ref.1) | copy-start | bytes 52
  34.1 52.1 %all-to-all-start.1 = ((bf16[16,80,128]{2,1,0:T(8,128)(2,1)}), bf16[16,80,128]{2,1,0:T(8,128)(2,1)S(1)}, u32[]{:S(2)}, u32[]{:S(2)}) async-start(bf16[16,80,128]{2,1,0:T(8,128)(2,1)} %prefix_second.1), calls=%async_computation.1 | async-start | bytes 655360 | tf_op jit(solution)/shard_map/all_to_all | solution.py:425
  101.9 4.7 %collective-permute-start.2 = (bf16[128,1024]{1,0:T(8,128)(2,1)S(1)}, bf16[128,1024]{1,0:T(8,128)(2,1)S(1)}, u32[]{:S(2)}, u32[]{:S(2)}) collective-permute-start(bf16[128,1024]{1,0:T(8,128)(2,1)S(1)} %bitcast.37), channel_id=1, source_target_pairs={{0,8},{8,0},{16,24},{24,16},{32,40},{40,32},{48,56},{56,48},{64,72... | collective-permute-start | bytes 786440 | tf_op jit(solution)/shard_map/ppermute | solution.py:433
